TPU v7x, 32 devices: a whole 2x2x4 slice. The times are simulated.
32 devices in a mesh: groups: 2 (over y), seq: 8 (over z, x), head: 2 (over core).
Axes of the slice: x: 2, y: 2, z: 4, core: 2. Of those that a mesh axis runs over, the one named last changes fastest.
Arguments:
- queries: bfloat16 [3072, 768], P(('groups', 'seq'), 'head'), parts along dimension 0, may hold values from -6 to 6
- key_input: bfloat16 [3072, 768], P(('groups', 'seq'), 'head'), parts along dimension 0, may hold values from -6 to 6
- value_input: bfloat16 [3072, 768], P(('groups', 'seq'), 'head'), parts along dimension 0, may hold values from -6 to 6
- grad_output: bfloat16 [3072, 768], P(('groups', 'seq'), 'head'), parts along dimension 0, may hold values from -6 to 6
- rand_blocks: int32 [48, 12, 3], P(('groups', 'seq'), 'head'), parts along dimension 0, may hold values from 0 to 23, as said below
- global_pos: int32 [512], P('groups'), parts along dimension 0, may hold values from 0 to 1535, as said below
Outputs:
- attended: bfloat16 [3072, 768], P(('groups', 'seq'), 'head'), parts along dimension 0
- query_grad: bfloat16 [3072, 768], P(('groups', 'seq'), 'head'), parts along dimension 0
- key_grad: bfloat16 [3072, 768], P(('groups', 'seq'), 'head'), parts along dimension 0
- value_grad: bfloat16 [3072, 768], P(('groups', 'seq'), 'head'), parts along dimension 0
There are 2 independent parts, one for each index of `groups`. A program takes and returns all parts, laid end to end along the dimension named above; each array names one. Nothing has to cross between parts.
Inputs may be any that keep to these rules, and one draw needn't show every extreme that they name: `rand_blocks`: entries are block numbers. For each seq shard of 3 query blocks and each group of heads g * 6 to g * 6 + 5, at most 7 of its 54 entries lie in one span of 3 blocks that starts at a multiple of 3, and exactly 7 in some span. `global_pos`: distinct positions; at most 64 of them lie in one span of 192 positions that starts at a multiple of 192, and exactly 64 in some span.
All inputs are finite; a program needn't handle non-finite values.
Results may differ from a plain program's by a relative error of at most 0.017.
Values may be sent and summed in bfloat16 or wider, within the bound.
No kernel may reach another device: no remote copies, remote signals or barrier semaphores. Data moves between devices by JAX's collectives and lax.ppermute only.
A program may use at most 64 MiB of HBM per device.

v0:
```python
import math

import jax
import jax.numpy as jnp
from jax import lax
from jax.sharding import PartitionSpec as P

HEAD_DIM = 64
BLOCK = 64
RAND = 3


MASKED = -1e30


def with_halo(array, sides, width):
    for axis, dim in sides:
        size, length = (lax.axis_size(axis), array.shape[dim])
        up = [(i, (i + 1) % size) for i in range(size - 1)]
        down = [(j, i) for i, j in up]
        last = lax.slice_in_dim(array, length - width, length, axis=dim)
        initial = lax.slice_in_dim(array, 0, width, axis=dim)
        before = lax.ppermute(last, axis, up)
        after = lax.ppermute(initial, axis, down)
        array = jnp.concatenate([before, array, after], axis=dim)
    return array


def attend_head(
    query, key_rows, value_rows, visible, global_keys, global_values, grad_out, score_scale
):
    local_score = (
        jnp.einsum("nqe,nke->nqk", query, key_rows, preferred_element_type=jnp.float32)
        * score_scale
    )
    local_score = jnp.where(visible, local_score, MASKED)
    global_score = (
        jnp.einsum("nqe,ke->nqk", query, global_keys, preferred_element_type=jnp.float32)
        * score_scale
    )
    highest = jnp.maximum(
        jnp.max(local_score, axis=-1, keepdims=True), jnp.max(global_score, axis=-1, keepdims=True)
    )
    local_exp = jnp.exp(local_score - highest)
    global_exp = jnp.exp(global_score - highest)
    totals = jnp.sum(local_exp, axis=-1, keepdims=True) + jnp.sum(
        global_exp, axis=-1, keepdims=True
    )
    local_weight = (local_exp / totals).astype(jnp.bfloat16)
    global_weight = (global_exp / totals).astype(jnp.bfloat16)
    outputs = (
        jnp.einsum("nqk,nke->nqe", local_weight, value_rows, preferred_element_type=jnp.float32)
        + jnp.einsum(
            "nqk,ke->nqe", global_weight, global_values, preferred_element_type=jnp.float32
        )
    ).astype(jnp.bfloat16)
    local_dp = jnp.einsum("nqe,nke->nqk", grad_out, value_rows, preferred_element_type=jnp.float32)
    global_dp = jnp.einsum(
        "nqe,ke->nqk", grad_out, global_values, preferred_element_type=jnp.float32
    )
    local_wf = local_weight.astype(jnp.float32)
    global_wf = global_weight.astype(jnp.float32)
    delta_sum = jnp.sum(local_wf * local_dp, axis=-1, keepdims=True) + jnp.sum(
        global_wf * global_dp, axis=-1, keepdims=True
    )
    local_ds = (local_wf * (local_dp - delta_sum) * score_scale).astype(jnp.bfloat16)
    global_ds = (global_wf * (global_dp - delta_sum) * score_scale).astype(jnp.bfloat16)
    grad_query = (
        jnp.einsum("nqk,nke->nqe", local_ds, key_rows, preferred_element_type=jnp.float32)
        + jnp.einsum("nqk,ke->nqe", global_ds, global_keys, preferred_element_type=jnp.float32)
    ).astype(jnp.bfloat16)
    local_dk = jnp.einsum("nqk,nqe->nke", local_ds, query, preferred_element_type=jnp.float32)
    local_dv = jnp.einsum(
        "nqk,nqe->nke", local_weight, grad_out, preferred_element_type=jnp.float32
    )
    global_dk = jnp.einsum("nqk,nqe->ke", global_ds, query, preferred_element_type=jnp.float32)
    global_dv = jnp.einsum(
        "nqk,nqe->ke", global_weight, grad_out, preferred_element_type=jnp.float32
    )
    return (outputs, grad_query, local_dk, local_dv, global_dk, global_dv, local_ds, local_weight)


def body(queries, key_input, value_input, grad_output, rand_blocks, global_pos):
    tokens = queries.shape[0]
    blocks = tokens // BLOCK
    head_count = queries.shape[1] // HEAD_DIM
    pair_width = 2 * HEAD_DIM
    shards = lax.axis_size("seq")
    own_index = lax.axis_index("seq")
    first_row = own_index * tokens
    score_scale = 1.0 / math.sqrt(HEAD_DIM)
    packed_kv = jnp.concatenate(
        (
            key_input.reshape(tokens, head_count, HEAD_DIM),
            value_input.reshape(tokens, head_count, HEAD_DIM),
        ),
        axis=2,
    )
    padded = with_halo(packed_kv, (("seq", 0),), BLOCK)
    window_kv = jnp.concatenate(
        [
            padded[offset * BLOCK : offset * BLOCK + tokens].reshape(
                blocks, BLOCK, head_count, pair_width
            )
            for offset in range(3)
        ],
        axis=1,
    ).transpose(2, 0, 1, 3)
    request_block = rand_blocks.reshape(-1)
    requests = request_block.shape[0]
    request_ids = jnp.arange(requests, dtype=jnp.int32)
    request_head = request_ids // RAND % head_count
    owner_shard = request_block // blocks
    capacity = max(2, (requests + shards - 1) // shards)
    slots_all = shards * capacity
    earlier = (owner_shard[:, None] == owner_shard[None, :]) & (
        request_ids[None, :] < request_ids[:, None]
    )
    slot_rank = jnp.sum(earlier.astype(jnp.int32), axis=1)
    request_slot = owner_shard * capacity + slot_rank
    slot_match = request_slot[None, :] == jnp.arange(slots_all, dtype=jnp.int32)[:, None]
    slot_used = jnp.any(slot_match, axis=1)
    slot_source = jnp.sum(jnp.where(slot_match, request_ids[None, :], 0), axis=1)
    request_code = request_block % blocks * head_count + request_head
    wanted = jnp.where(slot_used, jnp.take(request_code, slot_source), -1).reshape(shards, capacity)
    block_table = (
        packed_kv.reshape(blocks, BLOCK, head_count, pair_width)
        .transpose(0, 2, 1, 3)
        .reshape(blocks * head_count, BLOCK, pair_width)
    )
    asked_codes = lax.all_to_all(wanted, "seq", split_axis=0, concat_axis=0, tiled=True)
    picked = jnp.take(block_table, jnp.maximum(asked_codes, 0), axis=0)
    fetched, asked_codes = (
        lax.all_to_all(picked, "seq", split_axis=0, concat_axis=0, tiled=True),
        asked_codes,
    )
    random_kv = jnp.take(fetched.reshape(slots_all, BLOCK, pair_width), request_slot, axis=0)
    random_kv = random_kv.reshape(blocks, head_count, RAND * BLOCK, pair_width).transpose(
        1, 0, 2, 3
    )
    local_kv = jnp.concatenate((window_kv, random_kv), axis=2)
    block_ids = own_index * blocks + jnp.arange(blocks, dtype=jnp.int32)
    neighbour = block_ids[:, None] + jnp.arange(3, dtype=jnp.int32)[None, :] - 1
    inside = (neighbour >= 0) & (neighbour < blocks * shards)
    visible = jnp.concatenate(
        (jnp.repeat(inside, BLOCK, axis=1), jnp.ones((blocks, RAND * BLOCK), jnp.bool_)), axis=1
    )[:, None, :]
    global_count = global_pos.shape[0]
    global_ids = jnp.arange(global_count, dtype=jnp.int32)
    row_ids = jnp.arange(tokens, dtype=jnp.int32)
    flat_kv = packed_kv.reshape(tokens, head_count * pair_width)
    row_match = global_pos[:, None] == first_row + row_ids[None, :]
    partial_rows = jnp.dot(
        row_match.astype(jnp.bfloat16), flat_kv, preferred_element_type=jnp.float32
    )
    global_kv = lax.psum(partial_rows, "seq").astype(jnp.bfloat16)
    global_kv = global_kv.reshape(global_count, head_count, pair_width).transpose(1, 0, 2)

    def heads_first(array):
        return array.reshape(blocks, BLOCK, head_count, HEAD_DIM).transpose(2, 0, 1, 3)

    query_heads = heads_first(queries)
    grad_heads = heads_first(grad_output)

    def one_head(operands):
        query, local_pair, global_pair, grad_out = operands
        return attend_head(
            query,
            local_pair[..., :HEAD_DIM],
            local_pair[..., HEAD_DIM:],
            visible,
            global_pair[:, :HEAD_DIM],
            global_pair[:, HEAD_DIM:],
            grad_out,
            score_scale,
        )

    outputs, grad_query, local_dk, local_dv, global_dk, global_dv, local_ds, local_weight = lax.map(
        one_head, (query_heads, local_kv, global_kv, grad_heads)
    )

    def rows_last(array):
        return array.transpose(1, 2, 0, 3).reshape(tokens, head_count * HEAD_DIM)

    local_grad = jnp.concatenate((local_dk, local_dv), axis=3)
    window_grad = local_grad[:, :, : 3 * BLOCK].transpose(1, 2, 0, 3)
    spread = sum(
        (
            jnp.pad(
                window_grad[:, offset * BLOCK : (offset + 1) * BLOCK].reshape(
                    tokens, head_count, pair_width
                ),
                ((offset * BLOCK, (2 - offset) * BLOCK), (0, 0), (0, 0)),
            )
            for offset in range(3)
        )
    )
    rim_pair = jnp.concatenate((spread[:BLOCK], spread[-BLOCK:]), axis=0)
    rim_in = with_halo(rim_pair.astype(jnp.bfloat16), (("seq", 0),), BLOCK).astype(rim_pair.dtype)
    window_total = (
        spread[BLOCK:-BLOCK]
        + jnp.pad(rim_in[:BLOCK], ((0, tokens - BLOCK), (0, 0), (0, 0)))
        + jnp.pad(rim_in[-BLOCK:], ((tokens - BLOCK, 0), (0, 0), (0, 0)))
    )
    random_grad = local_grad[:, :, 3 * BLOCK :].reshape(head_count, blocks, RAND, BLOCK, pair_width)
    random_grad = (
        random_grad.transpose(1, 0, 2, 3, 4)
        .reshape(requests, BLOCK, pair_width)
        .astype(jnp.bfloat16)
    )
    outgoing = jnp.where(slot_used[:, None, None], jnp.take(random_grad, slot_source, axis=0), 0)
    returned = lax.all_to_all(
        outgoing.reshape(shards, capacity, BLOCK, pair_width),
        "seq",
        split_axis=0,
        concat_axis=0,
        tiled=True,
    )
    target = (
        asked_codes.reshape(-1)[None, :]
        == jnp.arange(blocks * head_count, dtype=jnp.int32)[:, None]
    ).astype(jnp.bfloat16)
    random_total = jnp.dot(
        target, returned.reshape(slots_all, BLOCK * pair_width), preferred_element_type=jnp.float32
    )
    random_total = (
        random_total.reshape(blocks, head_count, BLOCK, pair_width)
        .transpose(0, 2, 1, 3)
        .reshape(tokens, head_count, pair_width)
    )
    global_grad = (
        jnp.concatenate((global_dk, global_dv), axis=2)
        .transpose(1, 0, 2)
        .reshape(global_count, head_count * pair_width)
    )
    global_total = lax.psum(global_grad, "seq")
    row_source = jnp.sum(jnp.where(row_match, global_ids[:, None], 0), axis=0)
    row_used = jnp.any(row_match, axis=0)
    global_rows = jnp.where(row_used[:, None], jnp.take(global_total, row_source, axis=0), 0.0)
    grand_total = window_total + random_total + global_rows.reshape(tokens, head_count, pair_width)
    key_rows_out = (
        grand_total[..., :HEAD_DIM].reshape(tokens, head_count * HEAD_DIM).astype(jnp.bfloat16)
    )
    value_rows_out = (
        grand_total[..., HEAD_DIM:].reshape(tokens, head_count * HEAD_DIM).astype(jnp.bfloat16)
    )
    return (rows_last(outputs), rows_last(grad_query), key_rows_out, value_rows_out)


def solution(mesh):
    in_specs = (
        P(("groups", "seq"), "head"),
        P(("groups", "seq"), "head"),
        P(("groups", "seq"), "head"),
        P(("groups", "seq"), "head"),
        P(("groups", "seq"), "head", None),
        P("groups"),
    )
    out_specs = (
        P(("groups", "seq"), "head"),
        P(("groups", "seq"), "head"),
        P(("groups", "seq"), "head"),
        P(("groups", "seq"), "head"),
    )
    return jax.shard_map(body, mesh=mesh, in_specs=in_specs, out_specs=out_specs, check_vma=False)
```

profile of v0, /device:TPU:0, one launch (start us, length us, event | category | flops | bytes accessed | tf_op | source)
XLA Modules:
  0.0 263.8 jit_solution(7505868109951577211)
XLA Ops:
  11.4 7.3 %all-to-all-start = ((s32[8,1,7]{2,1,0:T(1,128)}), s32[8,1,7]{2,1,0:T(1,128)S(1)}, u32[]{:S(2)}, u32[]{:S(2)}) async-start(s32[8,1,7]{2,1,0:T(1,128)} %bitcast.24), calls=%async_computation | async-start | bytes 8192 | tf_op jit(solution)/shard_map/all_to_all | solution.py:131
  18.6 1.0 copy.132
  19.7 1.1 copy.133
  20.8 3.9 %collective-permute-start = (bf16[64,6,128]{0,2,1:T(8,128)(2,1)S(1)}, bf16[64,6,128]{0,2,1:T(8,128)(2,1)S(1)}, u32[]{:S(2)}, u32[]{:S(2)}) collective-permute-start(bf16[64,6,128]{0,2,1:T(8,128)(2,1)S(1)} %get-tuple-element.187), channel_id=1, source_target_pairs={{0,2},{2,4},{4,6},{6,8},{8,10},{10,12},{12,14},{1,3},{3,5},{5,7},{... | collective-permute-start | bytes 294920 | tf_op jit(solution)/shard_map/ppermute | solution.py:23
  24.8 1.3 collective-permute-start.1
  29.2 1.1 broadcast_select_fusion
  30.3 7.4 %all-to-all-start.1 = ((bf16[8,7,64,128]{3,2,1,0:T(8,128)(2,1)}), bf16[8,7,64,128]{3,2,1,0:T(8,128)(2,1)S(1)}, u32[]{:S(2)}, u32[]{:S(2)}) async-start(bf16[8,7,64,128]{3,2,1,0:T(8,128)(2,1)} %broadcast_select_fusion), calls=%async_computation.1 | async-start | bytes 1835008 | tf_op jit(solution)/shard_map/all_to_all | solution.py:134
  42.9 1.4 pad_maximum_fusion.3
  46.6 48.3 %all-reduce.9 = bf16[256,768]{1,0:T(8,128)(2,1)S(1)} all-reduce(f32[256,768]{1,0:T(8,128)S(1)} %fusion.63), channel_id=1, replica_groups=mesh['groups'=2,'seq'=8,'head'=2] {'seq'}, use_global_device_ids=true, to_apply=%region_3.4 | all-reduce | flops 196608 | bytes 1179648 | tf_op jit(solution)/shard_map/psum | solution.py:156
  95.8 1.3 maximum_bitcast_fusion
  97.1 1.7 gather_fusion.2
  98.8 1.6 fusion.56
  101.5 46.4 %while.20 = (s32[]{:T(128)}, bf16[6,3,64,64]{3,2,1,0:T(8,128)(2,1)S(1)}, bf16[6,3,64,64]{3,2,1,0:T(8,128)(2,1)}, f32[6,3,384,64]{2,3,1,0:T(8,128)}, f32[6,3,384,...) while((s32[]{:T(128)}, ...), condition=%wide.region_11.12_spmd, body=%wide.region_4.11_spmd.sunk | while | flops 96337344 | bytes 7745945 | solution.py:178
  128.3 1.0 fusion.161
  135.1 1.0 fusion.160
  136.0 1.0 fusion.161
  148.6 2.3 copy.156
  150.9 3.5 %copy.157 = f32[6,3,384,64]{3,2,1,0:T(8,128)} copy(f32[6,3,384,64]{2,3,1,0:T(8,128)} %get-tuple-element.74) | data formatting | bytes 3538944 | tf_op jit(solution)/shard_map/while | solution.py:178
  154.3 1.9 fusion.53
  156.2 1.0 copy.158
  157.2 2.9 %gather_fusion.3 = bf16[56,64,128]{2,1,0:T(8,128)(2,1)} fusion(bf16[54,64,128]{2,1,0:T(8,128)(2,1)} %bitcast.235, s32[1024]{0:T(1024)} %copy-done.12), kind=kCustom, calls=%fused_computation.3 | custom fusion | bytes 1835232 | tf_op jit(solution)/shard_map/jit(_take)/gather | solution.py:211
  160.1 2.3 select_select_fusion
  162.4 4.2 %all-to-all-start.2 = ((bf16[8,7,64,128]{3,2,1,0:T(8,128)(2,1)}), bf16[8,7,64,128]{3,2,1,0:T(8,128)(2,1)}, u32[]{:S(2)}, u32[]{:S(2)}) async-start(bf16[8,7,64,128]{3,2,1,0:T(8,128)(2,1)} %select_select_fusion), calls=%async_computation.2 | async-start | bytes 1835008 | tf_op jit(solution)/shard_map/all_to_all | solution.py:212
  166.7 2.1 pad_maximum_fusion.2
  168.8 2.3 copy.161
  171.2 2.0 fusion.52
  173.6 3.8 %collective-permute-start.2 = (bf16[64,6,128]{2,0,1:T(8,128)(2,1)S(1)}, bf16[64,6,128]{2,0,1:T(8,128)(2,1)S(1)}, u32[]{:S(2)}, u32[]{:S(2)}) collective-permute-start(bf16[64,6,128]{2,0,1:T(8,128)(2,1)S(1)} %get-tuple-element.182), channel_id=1, source_target_pairs={{0,2},{2,4},{4,6},{6,8},{8,10},{10,12},{12,14},{1,3},{3,5},{5,7},{... | collective-permute-start | bytes 294920 | tf_op jit(solution)/shard_map/ppermute | solution.py:23
  177.4 1.5 collective-permute-start.3
  182.4 1.5 collective-permute-done.3
  184.0 66.3 %all-reduce.8.cloned.1.call-done = f32[256,768]{1,0:T(8,128)} async-done(((f32[256,768]{1,0:T(8,128)}), f32[256,768]{1,0:T(8,128)}) %all-reduce.8.cloned.1.call-update) | async-done | bytes 786448 | tf_op jit(solution)/shard_map/psum | solution.py:236
  250.3 2.3 gather_fusion.4
  252.7 1.9 fusion.54
  (266 shorter events, 66.6 us)
Async XLA Ops:
  7.2 18.9 %copy-start.1 = (bf16[192,384]{1,0:T(8,128)(2,1)S(1)}, bf16[192,384]{1,0:T(8,128)(2,1)}, u32[]{:S(2)}) copy-start(bf16[192,384]{1,0:T(8,128)(2,1)} %param.9) | copy-start | bytes 442372
  7.2 19.2 %copy-start.2 = (bf16[192,384]{1,0:T(8,128)(2,1)S(1)}, bf16[192,384]{1,0:T(8,128)(2,1)}, u32[]{:S(2)}) copy-start(bf16[192,384]{1,0:T(8,128)(2,1)} %param.10) | copy-start | bytes 442372
  9.8 16.3 %copy-start.12 = (s32[1024]{0:T(1024)}, s32[1024]{0:T(1024)S(1)}, u32[]{:S(2)}) copy-start(s32[1024]{0:T(1024)S(1)} %pad_clamp_fusion.3) | copy-start | bytes 12292
  11.4 16.9 %all-to-all-start = ((s32[8,1,7]{2,1,0:T(1,128)}), s32[8,1,7]{2,1,0:T(1,128)S(1)}, u32[]{:S(2)}, u32[]{:S(2)}) async-start(s32[8,1,7]{2,1,0:T(1,128)} %bitcast.24), calls=%async_computation | async-start | bytes 8192 | tf_op jit(solution)/shard_map/all_to_all | solution.py:131
  19.7 7.3 %copy-start.10 = (s32[3,6,3]{1,2,0:T(4,128)S(1)}, s32[3,6,3]{1,2,0:T(4,128)}, u32[]{:S(2)}) copy-start(s32[3,6,3]{1,2,0:T(4,128)} %param.12) | copy-start | bytes 652
  20.8 6.7 %copy-start.11 = (s32[256]{0:T(256)S(1)}, s32[256]{0:T(256)}, u32[]{:S(2)}) copy-start(s32[256]{0:T(256)} %param.13) | copy-start | bytes 3076
  20.8 21.3 %collective-permute-start = (bf16[64,6,128]{0,2,1:T(8,128)(2,1)S(1)}, bf16[64,6,128]{0,2,1:T(8,128)(2,1)S(1)}, u32[]{:S(2)}, u32[]{:S(2)}) collective-permute-start(bf16[64,6,128]{0,2,1:T(8,128)(2,1)S(1)} %get-tuple-element.187), channel_id=1, source_target_pairs={{0,2},{2,4},{4,6},{6,8},{8,10},{10,12},{12,14},{1,3},{3,5},{5,7},{... | collective-permute-start | bytes 294920 | tf_op jit(solution)/shard_map/ppermute | solution.py:23
  24.8 18.1 %collective-permute-start.1 = (bf16[64,6,128]{0,2,1:T(8,128)(2,1)S(1)}, bf16[64,6,128]{0,2,1:T(8,128)(2,1)}, u32[]{:S(2)}, u32[]{:S(2)}) collective-permute-start(bf16[64,6,128]{0,2,1:T(8,128)(2,1)S(1)} %get-tuple-element.188), channel_id=1, source_target_pairs={{2,0},{4,2},{6,4},{8,6},{10,8},{12,10},{14,12},{3,1},{5,3},{7,5},{... | collective-permute-start | bytes 294920 | tf_op jit(solution)/shard_map/ppermute | solution.py:24
  29.2 10.3 %copy-start.8 = (bf16[192,384]{1,0:T(8,128)(2,1)S(1)}, bf16[192,384]{1,0:T(8,128)(2,1)}, u32[]{:S(2)}) copy-start(bf16[192,384]{1,0:T(8,128)(2,1)} %param.8) | copy-start | bytes 442372
  30.3 9.5 %copy-start.9 = (bf16[192,384]{1,0:T(8,128)(2,1)S(1)}, bf16[192,384]{1,0:T(8,128)(2,1)}, u32[]{:S(2)}) copy-start(bf16[192,384]{1,0:T(8,128)(2,1)} %param.11) | copy-start | bytes 442372
  30.3 66.8 %all-to-all-start.1 = ((bf16[8,7,64,128]{3,2,1,0:T(8,128)(2,1)}), bf16[8,7,64,128]{3,2,1,0:T(8,128)(2,1)S(1)}, u32[]{:S(2)}, u32[]{:S(2)}) async-start(bf16[8,7,64,128]{3,2,1,0:T(8,128)(2,1)} %broadcast_select_fusion), calls=%async_computation.1 | async-start | bytes 1835008 | tf_op jit(solution)/shard_map/all_to_all | solution.py:134
  41.0 5.6 %copy-start.14 = (s32[192]{0:T(256)}, s32[192]{0:T(256)S(1)}, u32[]{:S(2)}) copy-start(s32[192]{0:T(256)S(1)} %fusion.65) | copy-start | bytes 2308
  42.1 0.7 copy-start.7
  100.4 1.0 copy-start
  100.5 1.0 copy-start.3
  147.9 0.7 copy-start.4
  156.2 3.9 %copy-start.13 = (pred[8,7]{1,0:T(8,128)(4,1)S(1)}, pred[8,7]{1,0:T(8,128)(4,1)}, u32[]{:S(2)}) copy-start(pred[8,7]{1,0:T(8,128)(4,1)} %compare_and_fusion.2) | copy-start | bytes 172
  160.1 6.6 %copy-start.16 = (s32[192,1]{0,1:T(1,128)S(1)}, s32[192,1]{0,1:T(1,128)}, u32[]{:S(2)}) copy-start(s32[192,1]{0,1:T(1,128)} %compare_select_fusion.4) | copy-start | bytes 2308
  160.1 6.6 %copy-start.15 = (s32[192]{0:T(256)S(1)}, s32[192]{0:T(256)}, u32[]{:S(2)}) copy-start(s32[192]{0:T(256)} %copy-done.14) | copy-start | bytes 2308
  162.4 90.3 %all-to-all-start.2 = ((bf16[8,7,64,128]{3,2,1,0:T(8,128)(2,1)}), bf16[8,7,64,128]{3,2,1,0:T(8,128)(2,1)}, u32[]{:S(2)}, u32[]{:S(2)}) async-start(bf16[8,7,64,128]{3,2,1,0:T(8,128)(2,1)} %select_select_fusion), calls=%async_computation.2 | async-start | bytes 1835008 | tf_op jit(solution)/shard_map/all_to_all | solution.py:212
  166.7 83.7 %all-reduce.8.cloned.1.call-start = ((), (), s32[]{:S(2)}) async-start(), calls=%async_computation.3 | async-start | bytes 1572864 | tf_op jit(solution)/shard_map/psum | solution.py:236
  173.4 6.7 %copy-start.5 = (bf16[6,3,64,64]{3,2,1,0:T(8,128)(2,1)S(1)}, bf16[6,3,64,64]{3,2,1,0:T(8,128)(2,1)}, u32[]{:S(2)}) copy-start(bf16[6,3,64,64]{3,2,1,0:T(8,128)(2,1)} %copy-done.4) | copy-start | bytes 442372
  173.4 7.9 %copy-start.6 = (bf16[6,3,64,64]{3,2,1,0:T(8,128)(2,1)S(1)}, bf16[6,3,64,64]{3,2,1,0:T(8,128)(2,1)}, u32[]{:S(2)}) copy-start(bf16[6,3,64,64]{3,2,1,0:T(8,128)(2,1)} %get-tuple-element.72) | copy-start | bytes 442372
  173.6 8.8 %collective-permute-start.2 = (bf16[64,6,128]{2,0,1:T(8,128)(2,1)S(1)}, bf16[64,6,128]{2,0,1:T(8,128)(2,1)S(1)}, u32[]{:S(2)}, u32[]{:S(2)}) collective-permute-start(bf16[64,6,128]{2,0,1:T(8,128)(2,1)S(1)} %get-tuple-element.182), channel_id=1, source_target_pairs={{0,2},{2,4},{4,6},{6,8},{8,10},{10,12},{12,14},{1,3},{3,5},{5,7},{... | collective-permute-start | bytes 294920 | tf_op jit(solution)/shard_map/ppermute | solution.py:23
  177.4 6.5 %collective-permute-start.3 = (bf16[64,6,128]{2,0,1:T(8,128)(2,1)S(1)}, bf16[64,6,128]{2,0,1:T(8,128)(2,1)S(1)}, u32[]{:S(2)}, u32[]{:S(2)}) collective-permute-start(bf16[64,6,128]{2,0,1:T(8,128)(2,1)S(1)} %get-tuple-element.183), channel_id=1, source_target_pairs={{2,0},{4,2},{6,4},{8,6},{10,8},{12,10},{14,12},{3,1},{5,3},{7,5},{... | collective-permute-start | bytes 294920 | tf_op jit(solution)/shard_map/ppermute | solution.py:24
  184.0 70.6 %copy-start.17 = (pred[192]{0:T(512)(128)(4,1)S(1)}, pred[192]{0:T(512)(128)(4,1)}, u32[]{:S(2)}) copy-start(pred[192]{0:T(512)(128)(4,1)} %compare_reduce_fusion) | copy-start | bytes 580
  184.0 70.6 %copy-start.18 = (pred[192]{0:T(512)(128)(4,1)S(1)}, pred[192]{0:T(512)(128)(4,1)}, u32[]{:S(2)}) copy-start(pred[192]{0:T(512)(128)(4,1)} %constant.163.clone.1) | copy-start | bytes 580
Sparse Core Ops, SparseCore 0:
  171.3 78.9 all-reduce.7
where the time goes:
time: 265 us; the launch traced here: 264 us
  waiting for transfers between devices  67.8 us (26%)
  blocking collectives  48.3 us (18%)
  local copies, waits for them, and re-layouts  40.9 us (15%)
  matrix products  38 us (14%)
  starting transfers between devices  29.4 us (11%)
  other arithmetic  24.2 us (9%)
  between operations  14.7 us (6%)
    psum x1, waiting for transfers between devices, body(): global_total = lax.psum(global_grad, 'seq')  66.3 us
    psum x1, blocking collectives, body(): global_kv = lax.psum(partial_rows, 'seq').astype(jnp.bfloat16)  48.3 us
    ppermute x2, starting transfers between devices, with_halo(): before = lax.ppermute(last, axis, up)  7.69 us
    all_to_all x1, starting transfers between devices, body(): lax.all_to_all(picked, 'seq', split_axis=0, concat_axis=0, tiled=True)  7.39 us
    all_to_all x1, starting transfers between devices, body(): lax.all_to_all(wanted, 'seq', split_axis=0, concat_axis=0, tiled=True)  7.25 us
    while x4, local copies, waits for them, and re-layouts, body(): lax.map(one_head, (query_heads, local_kv, global_kv, grad_heads))  6.57 us
    unnamed x42, local copies, waits for them, and re-layouts  6.06 us
    dot_general x6, matrix products, attend_head(): jnp.einsum('nqk,nqe->nke', local_ds, query, preferred_element_type=jnp.fl...  5.75 us
  transfers between devices with their start and end apart: 8, of which 2 were waited for; matrix products, arithmetic and copies ran while one was open for 11% of the time, Pallas kernels for 0%

commit v1 on v0

--- a/solution.py
+++ b/solution.py
@@ -1,8 +1,11 @@
+import functools
 import math
 
 import jax
 import jax.numpy as jnp
 from jax import lax
+from jax.experimental import pallas as pl
+from jax.experimental.pallas import tpu as pltpu
 from jax.sharding import PartitionSpec as P
 
 HEAD_DIM = 64
@@ -80,7 +83,7 @@
     return (outputs, grad_query, local_dk, local_dv, global_dk, global_dv, local_ds, local_weight)
 
 
-def body(queries, key_input, value_input, grad_output, rand_blocks, global_pos):
+def sparse_body(queries, key_input, value_input, grad_output, rand_blocks, global_pos):
     tokens = queries.shape[0]
     blocks = tokens // BLOCK
     head_count = queries.shape[1] // HEAD_DIM
@@ -247,6 +250,250 @@
     return (rows_last(outputs), rows_last(grad_query), key_rows_out, value_rows_out)
 
 
+DENSE_ROWS = 4096
+VMEM_BYTES = 48 * 1024 * 1024
+
+
+def dot(left, right, left_dim, right_dim):
+    return lax.dot_general(
+        left,
+        right,
+        (((left_dim,), (right_dim,)), ((), ())),
+        preferred_element_type=jnp.float32,
+    )
+
+
+def pack_kernel(first_ref, second_ref, packed_ref):
+    heads = first_ref.shape[1] // HEAD_DIM
+    for head in range(heads):
+        cols = slice(head * HEAD_DIM, (head + 1) * HEAD_DIM)
+        packed_ref[:, 2 * head * HEAD_DIM : 2 * (head + 1) * HEAD_DIM] = jnp.concatenate(
+            (first_ref[:, cols], second_ref[:, cols]), axis=1
+        )
+
+
+def rows_kernel(query_ref, grad_ref, rows_ref):
+    heads, rows, _ = rows_ref.shape
+    zeros = jnp.zeros((BLOCK, HEAD_DIM), jnp.bfloat16)
+    for head in range(heads):
+        cols = slice(head * HEAD_DIM, (head + 1) * HEAD_DIM)
+        for block in range(rows // (2 * BLOCK)):
+            at = slice(block * BLOCK, (block + 1) * BLOCK)
+            query = query_ref[at, cols] * jnp.bfloat16(1.0 / math.sqrt(HEAD_DIM))
+            base = 2 * block * BLOCK
+            rows_ref[head, base : base + BLOCK, :] = jnp.concatenate((query, zeros), axis=1)
+            rows_ref[head, base + BLOCK : base + 2 * BLOCK, :] = jnp.concatenate(
+                (zeros, grad_ref[at, cols]), axis=1
+            )
+
+
+def unpack_kernel(*refs):
+    *packed_refs, first_ref, second_ref = refs
+    heads = first_ref.shape[1] // HEAD_DIM
+    for head in range(heads):
+        wide = slice(2 * head * HEAD_DIM, 2 * (head + 1) * HEAD_DIM)
+        total = packed_refs[0][:, wide].astype(jnp.float32)
+        for ref in packed_refs[1:]:
+            total = total + ref[:, wide].astype(jnp.float32)
+        total = total.astype(jnp.bfloat16)
+        cols = slice(head * HEAD_DIM, (head + 1) * HEAD_DIM)
+        first_ref[:, cols] = total[:, :HEAD_DIM]
+        second_ref[:, cols] = total[:, HEAD_DIM:]
+
+
+def shard_of(own, steps, mate, lines):
+    line_pos = lax.rem(own // 2 + steps + lines, lines)
+    side = own % 2
+    return 2 * line_pos + (1 - side if mate else side)
+
+
+def attend_kernel(shards, rand_ref, pos_row_ref, pos_col_ref, rows_ref, *refs):
+    pieces = refs[:shards]
+    packed_ref = refs[shards]
+    chunks = refs[shards + 1 : 2 * shards + 1]
+    kv, acc, global_kv, global_acc, sems = refs[2 * shards + 1 :]
+    tokens = packed_ref.shape[0]
+    blocks = tokens // BLOCK
+    heads = rows_ref.shape[0]
+    global_count = pos_row_ref.shape[1]
+    lines = shards // 2
+    own = lax.axis_index("seq")
+
+    def rows_at(shard):
+        return pl.ds(pl.multiple_of(shard * tokens, BLOCK), tokens)
+
+    copies = []
+    for slot in range(shards):
+        source = shard_of(own, -(slot % lines), slot >= lines, lines)
+        copies.append(
+            pltpu.make_async_copy(pieces[slot], kv.at[rows_at(source)], sems.at[slot])
+        )
+    for copy in copies:
+        copy.start()
+    acc[...] = jnp.zeros_like(acc)
+    position = lax.broadcasted_iota(jnp.int32, (global_count, shards * tokens), 1)
+    pick = (position == pos_col_ref[...]).astype(jnp.bfloat16)
+    for copy in copies:
+        copy.wait()
+    global_kv[...] = dot(pick, kv[...], 1, 0).astype(jnp.bfloat16)
+    lane = lax.broadcasted_iota(jnp.int32, (BLOCK, 6 * BLOCK), 1)
+    half = lax.broadcasted_iota(jnp.int32, (BLOCK, 2 * HEAD_DIM), 1) < HEAD_DIM
+
+    def one_head(head, carry):
+        cols = pl.ds(pl.multiple_of(head * 2 * HEAD_DIM, 2 * HEAD_DIM), 2 * HEAD_DIM)
+        gkv = global_kv[:, cols]
+        rows = rows_ref[head]
+        global_dots = dot(rows, gkv, 1, 1)
+        global_sides = []
+        for block in range(blocks):
+            here = own * blocks + block
+            places = [
+                jnp.maximum(here - 1, 0),
+                here,
+                jnp.minimum(here + 1, shards * blocks - 1),
+            ] + [rand_ref[(block * heads + head) * RAND + r] for r in range(RAND)]
+            places = [pl.ds(pl.multiple_of(p * BLOCK, BLOCK), BLOCK) for p in places]
+            local_kv = jnp.concatenate([kv[p, cols] for p in places], axis=0)
+            base = 2 * block * BLOCK
+            both = rows[base : base + 2 * BLOCK]
+            local_dots = dot(both, local_kv, 1, 1)
+            score, dp = local_dots[:BLOCK], local_dots[BLOCK:]
+            if block == 0:
+                score = jnp.where((lane < BLOCK) & (here == 0), MASKED, score)
+            if block == blocks - 1:
+                outside = (lane >= 2 * BLOCK) & (lane < 3 * BLOCK)
+                score = jnp.where(outside & (here == shards * blocks - 1), MASKED, score)
+            global_score = global_dots[base : base + BLOCK]
+            global_dp = global_dots[base + BLOCK : base + 2 * BLOCK]
+            highest = jnp.maximum(
+                jnp.max(score, axis=1, keepdims=True),
+                jnp.max(global_score, axis=1, keepdims=True),
+            )
+            local_exp = jnp.exp(score - highest)
+            global_exp = jnp.exp(global_score - highest)
+            inverse = 1.0 / (
+                jnp.sum(local_exp, axis=1, keepdims=True)
+                + jnp.sum(global_exp, axis=1, keepdims=True)
+            )
+            local_weight = (local_exp * inverse).astype(jnp.bfloat16)
+            global_weight = (global_exp * inverse).astype(jnp.bfloat16)
+            local_wf = local_weight.astype(jnp.float32)
+            global_wf = global_weight.astype(jnp.float32)
+            delta = jnp.sum(local_wf * dp, axis=1, keepdims=True) + jnp.sum(
+                global_wf * global_dp, axis=1, keepdims=True
+            )
+            local_ds = (local_wf * (dp - delta)).astype(jnp.bfloat16)
+            global_ds = (global_wf * (global_dp - delta)).astype(jnp.bfloat16)
+            local_side = jnp.concatenate((local_ds, local_weight), axis=0)
+            global_side = jnp.concatenate((global_ds, global_weight), axis=0)
+            global_sides.append(global_side)
+            result = dot(local_side, local_kv, 1, 0) + dot(global_side, gkv, 1, 0)
+            packed_ref[block * BLOCK : (block + 1) * BLOCK, cols] = jnp.where(
+                half, result[:BLOCK] * (1.0 / math.sqrt(HEAD_DIM)), result[BLOCK:]
+            ).astype(jnp.bfloat16)
+            local_grad = dot(local_side, both, 0, 0)
+            for i, place in enumerate(places):
+                acc[place, cols] += local_grad[i * BLOCK : (i + 1) * BLOCK]
+        global_acc[:, cols] = dot(jnp.concatenate(global_sides, axis=0), rows, 0, 0).astype(
+            jnp.bfloat16
+        )
+        return carry
+
+    lax.fori_loop(0, heads, one_head, 0)
+    for slot in range(shards):
+        target = shard_of(own, slot % lines, slot >= lines, lines)
+        position = target * tokens + lax.broadcasted_iota(jnp.int32, (tokens, global_count), 0)
+        spread = (position == pos_row_ref[...]).astype(jnp.bfloat16)
+        chunks[slot][...] = (
+            acc[rows_at(target)] + dot(spread, global_acc[...], 1, 0)
+        ).astype(jnp.bfloat16)
+
+
+def dense_body(queries, key_input, value_input, grad_output, rand_blocks, global_pos):
+    tokens, width = queries.shape
+    heads = width // HEAD_DIM
+    shards = lax.axis_size("seq")
+    lines = shards // 2
+    global_count = global_pos.shape[0]
+    bf16 = jnp.bfloat16
+    params = pltpu.CompilerParams(vmem_limit_bytes=VMEM_BYTES)
+    wide = jax.ShapeDtypeStruct((tokens, 2 * width), bf16)
+    narrow = jax.ShapeDtypeStruct((tokens, width), bf16)
+
+    def along(array, steps):
+        pairs = [(s, (s // 2 + steps) % lines * 2 + s % 2) for s in range(shards)]
+        return lax.ppermute(array, "seq", pairs)
+
+    def across(array):
+        return lax.ppermute(array, "seq", [(s, s ^ 1) for s in range(shards)])
+
+    def pack(first, second):
+        return pl.pallas_call(pack_kernel, out_shape=wide, compiler_params=params)(first, second)
+
+    def unpack(*packed):
+        return pl.pallas_call(unpack_kernel, out_shape=(narrow, narrow), compiler_params=params)(
+            *packed
+        )
+
+    near_first = sorted(range(1, lines), key=lambda k: min(k, lines - k))
+    kv = pack(key_input, value_input)
+    own_line = [kv] + [None] * (lines - 1)
+    mate_line = [across(kv)] + [None] * (lines - 1)
+    for steps in near_first:
+        own_line[steps] = along(kv, steps)
+    for steps in near_first:
+        mate_line[steps] = across(own_line[steps])
+    rows = pl.pallas_call(
+        rows_kernel,
+        out_shape=jax.ShapeDtypeStruct((heads, 2 * tokens, 2 * HEAD_DIM), bf16),
+        compiler_params=params,
+        cost_estimate=pl.CostEstimate(flops=0, bytes_accessed=6 * tokens * width, transcendentals=0),
+    )(queries, grad_output)
+    vmem = pl.BlockSpec(memory_space=pltpu.VMEM)
+    packed, *chunks = pl.pallas_call(
+        functools.partial(attend_kernel, shards),
+        out_shape=(wide,) * (shards + 1),
+        in_specs=[pl.BlockSpec(memory_space=pltpu.SMEM)]
+        + [vmem] * 3
+        + [pl.BlockSpec(memory_space=pl.ANY)] * shards,
+        out_specs=(vmem,) * (shards + 1),
+        scratch_shapes=[
+            pltpu.VMEM((shards * tokens, 2 * width), bf16),
+            pltpu.VMEM((shards * tokens, 2 * width), jnp.float32),
+            pltpu.VMEM((global_count, 2 * width), bf16),
+            pltpu.VMEM((global_count, 2 * width), bf16),
+            pltpu.SemaphoreType.DMA((shards,)),
+        ],
+        compiler_params=params,
+    )(
+        rand_blocks.reshape(-1),
+        global_pos.reshape(1, -1),
+        global_pos.reshape(-1, 1),
+        rows,
+        *own_line,
+        *mate_line,
+    )
+    far_first = near_first[::-1]
+    from_mate = {steps: across(chunks[lines + steps]) for steps in far_first + [0]}
+    sent = [
+        along(
+            (chunks[steps].astype(jnp.float32) + from_mate[steps].astype(jnp.float32)).astype(bf16),
+            steps,
+        )
+        for steps in far_first
+    ]
+    query_grad, attended = unpack(packed)
+    key_grad, value_grad = unpack(chunks[0], from_mate[0], *sent)
+    return attended, query_grad, key_grad, value_grad
+
+
+def body(queries, *others):
+    shards = lax.axis_size("seq")
+    if shards % 2 == 0 and shards * queries.shape[0] <= DENSE_ROWS:
+        return dense_body(queries, *others)
+    return sparse_body(queries, *others)
+
+
 def solution(mesh):
     in_specs = (
         P(("groups", "seq"), "head"),

time: 265 us -> 97.1 us (0.37)
  blocking collectives: 48.3 us -> 0 us
  local copies, waits for them, and re-layouts: 40.9 us -> 2.16 us
  matrix products: 38 us -> 0 us
  other arithmetic: 24.2 us -> 0.22 us
  Pallas kernels: 0 us -> 16.4 us
  starting transfers between devices: 29.4 us -> 15.4 us
  between operations: 14.7 us -> 0.78 us
  waiting for transfers between devices: 67.8 us -> 61.9 us
    psum x1 -> x0, waiting for transfers between devices: 66.3 us -> none  [body(): global_total = lax.psum(global_grad, 'seq')]
    ppermute x4 -> x14, waiting for transfers between devices: 1.49 us -> 61.9 us  [the longest x8 33.2 us: across(): return lax.ppermute(array, 'seq', [(s, s ^ 1) for s in range(shards)])]
    psum x1 -> x0, blocking collectives: 48.3 us -> none  [body(): global_kv = lax.psum(partial_rows, 'seq').astype(jnp.bfloat16)]
    dot_general x74 -> x0, matrix products: 38 us -> none  [the longest x6 5.75 us: attend_head(): jnp.einsum('nqk,nqe->nke', local_ds, query, preferred_element_type=jnp.fl...]
    all_to_all x3 -> x0, starting transfers between devices: 18.9 us -> none  [the longest x1 7.39 us: body(): lax.all_to_all(picked, 'seq', split_axis=0, concat_axis=0, tiled=True)]
    pallas_call x0 -> x5, Pallas kernels: none -> 16.4 us  [the longest x1 14.3 us: dense_body(): pl.pallas_call(functools.partial(attend_kernel, shards), out_shape=(wide,...]
    gather x6 -> x0, local copies, waits for them, and re-layouts: 8.52 us -> none  [the longest x1 2.89 us: body(): jnp.take(random_grad, slot_source, axis=0)]
    while x4 -> x0, local copies, waits for them, and re-layouts: 6.57 us -> none  [body(): lax.map(one_head, (query_heads, local_kv, global_kv, grad_heads))]
  transfers between devices with their start and end apart: 8 -> 14, of which waited for: 2 -> 8; matrix products, arithmetic and copies ran while one was open for 11% -> 1% of each run, Pallas kernels for 0% -> 1%
where the time goes in v1:
time: 97.1 us; the launch traced here: 96.9 us
  waiting for transfers between devices  61.9 us (64%)
  Pallas kernels  16.4 us (17%)
  starting transfers between devices  15.4 us (16%)
  local copies, waits for them, and re-layouts  2.16 us (2%)
    ppermute x8, waiting for transfers between devices, across(): return lax.ppermute(array, 'seq', [(s, s ^ 1) for s in range(shards)])  33.2 us
    ppermute x6, waiting for transfers between devices, along(): return lax.ppermute(array, 'seq', pairs)  28.7 us
    pallas_call x1, Pallas kernels, dense_body(): pl.pallas_call(functools.partial(attend_kernel, shards), out_shape=(wide,...  14.3 us
    ppermute x8, starting transfers between devices, across(): return lax.ppermute(array, 'seq', [(s, s ^ 1) for s in range(shards)])  9.13 us
    ppermute x6, starting transfers between devices, along(): return lax.ppermute(array, 'seq', pairs)  6.3 us
  transfers between devices with their start and end apart: 14, of which 8 were waited for; matrix products, arithmetic and copies ran while one was open for 1% of the time, Pallas kernels for 1%

profile of v1, /device:TPU:0, one launch (start us, length us, event | category | flops | bytes accessed | tf_op | source)
XLA Modules:
  0.0 96.9 jit_solution(4243961653505068454)
XLA Ops:
  0.6 0.9 copy-done.2
  1.5 0.9 copy-done.3
  2.5 0.1 shard_map.94.refs_0_
  2.6 5.1 %collective-permute-start.2 = (bf16[192,768]{1,0:T(8,128)(2,1)S(1)}, bf16[192,768]{1,0:T(8,128)(2,1)S(1)}, u32[]{:S(2)}, u32[]{:S(2)}) collective-permute-start(bf16[192,768]{1,0:T(8,128)(2,1)S(1)} %shard_map.94.refs_0_), channel_id=1, source_target_pairs={{0,12},{2,14},{4,0},{6,2},{8,4},{10,6},{12,8},{14,10},{1,13},{3,15... | collective-permute-start | bytes 884744 | tf_op jit(solution)/shard_map/ppermute | solution.py:425
  7.7 1.0 %collective-permute-start = (bf16[192,768]{1,0:T(8,128)(2,1)S(1)}, bf16[192,768]{1,0:T(8,128)(2,1)S(1)}, u32[]{:S(2)}, u32[]{:S(2)}) collective-permute-start(bf16[192,768]{1,0:T(8,128)(2,1)S(1)} %shard_map.94.refs_0_), channel_id=1, source_target_pairs={{0,4},{2,6},{4,8},{6,10},{8,12},{10,14},{12,0},{14,2},{1,5},{3,7},... | collective-permute-start | bytes 884744 | tf_op jit(solution)/shard_map/ppermute | solution.py:425
  8.7 1.5 %collective-permute-start.3 = (bf16[192,768]{1,0:T(8,128)(2,1)S(1)}, bf16[192,768]{1,0:T(8,128)(2,1)S(1)}, u32[]{:S(2)}, u32[]{:S(2)}) collective-permute-start(bf16[192,768]{1,0:T(8,128)(2,1)S(1)} %shard_map.94.refs_0_), channel_id=1, source_target_pairs={{0,2},{2,0},{4,6},{6,4},{8,10},{10,8},{12,14},{14,12},{1,3},{3,1},... | collective-permute-start | bytes 884744 | tf_op jit(solution)/shard_map/ppermute | solution.py:428
  10.2 5.0 %collective-permute-done.2.refs_3_ = bf16[192,768]{1,0:T(8,128)(2,1)S(1)} collective-permute-done((bf16[192,768]{1,0:T(8,128)(2,1)S(1)}, bf16[192,768]{1,0:T(8,128)(2,1)S(1)}, u32[]{:S(2)}, u32[]{:S(2)}) %collective-permute-start.2) | collective-permute-done | bytes 294944 | tf_op jit(solution)/shard_map/ppermute | solution.py:425
  15.2 1.5 %collective-permute-start.6 = (bf16[192,768]{1,0:T(8,128)(2,1)S(1)}, bf16[192,768]{1,0:T(8,128)(2,1)S(1)}, u32[]{:S(2)}, u32[]{:S(2)}) collective-permute-start(bf16[192,768]{1,0:T(8,128)(2,1)S(1)} %collective-permute-done.2.refs_3_), channel_id=1, source_target_pairs={{0,2},{2,0},{4,6},{6,4},{8,10},{10,8},{12,14},{14,12},{1,3},{3,1},... | collective-permute-start | bytes 884744 | tf_op jit(solution)/shard_map/ppermute | solution.py:428
  16.7 16.2 %collective-permute-done.1.refs_2_ = bf16[192,768]{1,0:T(8,128)(2,1)S(1)} collective-permute-done((bf16[192,768]{1,0:T(8,128)(2,1)S(1)}, bf16[192,768]{1,0:T(8,128)(2,1)S(1)}, u32[]{:S(2)}, u32[]{:S(2)}) %collective-permute-start.1) | collective-permute-done | bytes 294944 | tf_op jit(solution)/shard_map/ppermute | solution.py:425
  32.8 1.5 %collective-permute-start.5 = (bf16[192,768]{1,0:T(8,128)(2,1)S(1)}, bf16[192,768]{1,0:T(8,128)(2,1)S(1)}, u32[]{:S(2)}, u32[]{:S(2)}) collective-permute-start(bf16[192,768]{1,0:T(8,128)(2,1)S(1)} %collective-permute-done.1.refs_2_), channel_id=1, source_target_pairs={{0,2},{2,0},{4,6},{6,4},{8,10},{10,8},{12,14},{14,12},{1,3},{3,1},... | collective-permute-start | bytes 884744 | tf_op jit(solution)/shard_map/ppermute | solution.py:428
  34.3 0.5 collective-permute-start.4
  34.9 0.1 copy.11
  35.0 0.1 reshape.17.rand_ref
  35.1 0.1 copy.12.pos_col_ref
  35.2 0.2 shard_map.93.rows_ref
  35.4 7.4 %collective-permute-done.5.refs_6_ = bf16[192,768]{1,0:T(8,128)(2,1)S(1)} collective-permute-done((bf16[192,768]{1,0:T(8,128)(2,1)S(1)}, bf16[192,768]{1,0:T(8,128)(2,1)S(1)}, u32[]{:S(2)}, u32[]{:S(2)}) %collective-permute-start.5) | collective-permute-done | bytes 294944 | tf_op jit(solution)/shard_map/ppermute | solution.py:428
  42.8 4.3 %collective-permute-done.4.refs_5_ = bf16[192,768]{1,0:T(8,128)(2,1)S(1)} collective-permute-done((bf16[192,768]{1,0:T(8,128)(2,1)S(1)}, bf16[192,768]{1,0:T(8,128)(2,1)S(1)}, u32[]{:S(2)}, u32[]{:S(2)}) %collective-permute-start.4) | collective-permute-done | bytes 294944 | tf_op jit(solution)/shard_map/ppermute | solution.py:428
  47.0 14.3 %shard_map.95 = (bf16[192,768]{1,0:T(8,128)(2,1)S(1)}, bf16[192,768]{1,0:T(8,128)(2,1)S(1)}, bf16[192,768]{1,0:T(8,128)(2,1)S(1)}, bf16[192,768]{1,0:T(8,128)(2,...) custom-call(s32[54]{0:T(128)S(1)} %reshape.17.rand_ref, ...), custom_call_target="tpu_custom_call" | custom-call | tf_op jit(solution)/shard_map/pallas_call | solution.py:453
  61.3 1.6 %collective-permute-start.8 = (bf16[192,768]{1,0:T(8,128)(2,1)S(1)}, bf16[192,768]{1,0:T(8,128)(2,1)S(1)}, u32[]{:S(2)}, u32[]{:S(2)}) collective-permute-start(bf16[192,768]{1,0:T(8,128)(2,1)S(1)} %get-tuple-element.23), channel_id=1, source_target_pairs={{0,2},{2,0},{4,6},{6,4},{8,10},{10,8},{12,14},{14,12},{1,3},{3,1},... | collective-permute-start | bytes 884744 | tf_op jit(solution)/shard_map/ppermute | solution.py:428
  62.9 0.5 collective-permute-start.10
  63.4 1.5 %collective-permute-start.7 = (bf16[192,768]{1,0:T(8,128)(2,1)S(1)}, bf16[192,768]{1,0:T(8,128)(2,1)S(1)}, u32[]{:S(2)}, u32[]{:S(2)}) collective-permute-start(bf16[192,768]{1,0:T(8,128)(2,1)S(1)} %get-tuple-element.21), channel_id=1, source_target_pairs={{0,2},{2,0},{4,6},{6,4},{8,10},{10,8},{12,14},{14,12},{1,3},{3,1},... | collective-permute-start | bytes 884744 | tf_op jit(solution)/shard_map/ppermute | solution.py:428
  64.9 0.5 collective-permute-start.12
  65.4 5.9 %collective-permute-done.8 = bf16[192,768]{1,0:T(8,128)(2,1)S(1)} collective-permute-done((bf16[192,768]{1,0:T(8,128)(2,1)S(1)}, bf16[192,768]{1,0:T(8,128)(2,1)S(1)}, u32[]{:S(2)}, u32[]{:S(2)}) %collective-permute-start.8) | collective-permute-done | bytes 294944 | tf_op jit(solution)/shard_map/ppermute | solution.py:428
  71.3 0.1 add_convert_fusion.2
  71.4 0.1 collective-permute-start.9
  71.5 6.2 %collective-permute-done.10 = bf16[192,768]{1,0:T(8,128)(2,1)S(1)} collective-permute-done((bf16[192,768]{1,0:T(8,128)(2,1)S(1)}, bf16[192,768]{1,0:T(8,128)(2,1)S(1)}, u32[]{:S(2)}, u32[]{:S(2)}) %collective-permute-start.10) | collective-permute-done | bytes 294944 | tf_op jit(solution)/shard_map/ppermute | solution.py:428
  77.7 0.1 add_convert_fusion.1
  77.8 9.5 %collective-permute-done.12 = bf16[192,768]{1,0:T(8,128)(2,1)S(1)} collective-permute-done((bf16[192,768]{1,0:T(8,128)(2,1)S(1)}, bf16[192,768]{1,0:T(8,128)(2,1)S(1)}, u32[]{:S(2)}, u32[]{:S(2)}) %collective-permute-start.12) | collective-permute-done | bytes 294944 | tf_op jit(solution)/shard_map/ppermute | solution.py:428
  87.3 0.1 add_convert_fusion
  87.5 0.9 shard_map.96
  88.4 7.6 %collective-permute-done.13.refs_4_ = bf16[192,768]{1,0:T(8,128)(2,1)S(1)} collective-permute-done((bf16[192,768]{1,0:T(8,128)(2,1)S(1)}, bf16[192,768]{1,0:T(8,128)(2,1)S(1)}, u32[]{:S(2)}, u32[]{:S(2)}) %collective-permute-start.13) | collective-permute-done | bytes 294944 | tf_op jit(solution)/shard_map/ppermute | solution.py:425
  96.0 0.9 shard_map.97
  (19 shorter events, 0.2 us)
Async XLA Ops:
  0.6 0.9 copy-start.2
  1.5 0.9 copy-start.3
  2.5 32.4 %copy-start.5 = (s32[3,6,3]{1,2,0:T(4,128)S(1)}, s32[3,6,3]{1,2,0:T(4,128)}, u32[]{:S(2)}) copy-start(s32[3,6,3]{1,2,0:T(4,128)} %param.10) | copy-start | bytes 652
  2.5 32.6 %copy-start.4 = (s32[256]{0:T(256)S(1)}, s32[256]{0:T(256)}, u32[]{:S(2)}) copy-start(s32[256]{0:T(256)} %param.11) | copy-start | bytes 3076
  2.5 32.8 %copy-start.1 = (bf16[192,384]{1,0:T(8,128)(2,1)S(1)}, bf16[192,384]{1,0:T(8,128)(2,1)}, u32[]{:S(2)}) copy-start(bf16[192,384]{1,0:T(8,128)(2,1)} %grad_ref.1) | copy-start | bytes 442372
  2.6 32.6 %copy-start = (bf16[192,384]{1,0:T(8,128)(2,1)S(1)}, bf16[192,384]{1,0:T(8,128)(2,1)}, u32[]{:S(2)}) copy-start(bf16[192,384]{1,0:T(8,128)(2,1)} %query_ref.1) | copy-start | bytes 442372
  2.6 12.6 %collective-permute-start.2 = (bf16[192,768]{1,0:T(8,128)(2,1)S(1)}, bf16[192,768]{1,0:T(8,128)(2,1)S(1)}, u32[]{:S(2)}, u32[]{:S(2)}) collective-permute-start(bf16[192,768]{1,0:T(8,128)(2,1)S(1)} %shard_map.94.refs_0_), channel_id=1, source_target_pairs={{0,12},{2,14},{4,0},{6,2},{8,4},{10,6},{12,8},{14,10},{1,13},{3,15... | collective-permute-start | bytes 884744 | tf_op jit(solution)/shard_map/ppermute | solution.py:425
  7.7 25.1 %collective-permute-start.1 = (bf16[192,768]{1,0:T(8,128)(2,1)S(1)}, bf16[192,768]{1,0:T(8,128)(2,1)S(1)}, u32[]{:S(2)}, u32[]{:S(2)}) collective-permute-start(bf16[192,768]{1,0:T(8,128)(2,1)S(1)} %shard_map.94.refs_0_), channel_id=1, source_target_pairs={{0,8},{2,10},{4,12},{6,14},{8,0},{10,2},{12,4},{14,6},{1,9},{3,11}... | collective-permute-start | bytes 884744 | tf_op jit(solution)/shard_map/ppermute | solution.py:425
  7.7 26.6 %collective-permute-start = (bf16[192,768]{1,0:T(8,128)(2,1)S(1)}, bf16[192,768]{1,0:T(8,128)(2,1)S(1)}, u32[]{:S(2)}, u32[]{:S(2)}) collective-permute-start(bf16[192,768]{1,0:T(8,128)(2,1)S(1)} %shard_map.94.refs_0_), channel_id=1, source_target_pairs={{0,4},{2,6},{4,8},{6,10},{8,12},{10,14},{12,0},{14,2},{1,5},{3,7},... | collective-permute-start | bytes 884744 | tf_op jit(solution)/shard_map/ppermute | solution.py:425
  8.7 26.7 %collective-permute-start.3 = (bf16[192,768]{1,0:T(8,128)(2,1)S(1)}, bf16[192,768]{1,0:T(8,128)(2,1)S(1)}, u32[]{:S(2)}, u32[]{:S(2)}) collective-permute-start(bf16[192,768]{1,0:T(8,128)(2,1)S(1)} %shard_map.94.refs_0_), channel_id=1, source_target_pairs={{0,2},{2,0},{4,6},{6,4},{8,10},{10,8},{12,14},{14,12},{1,3},{3,1},... | collective-permute-start | bytes 884744 | tf_op jit(solution)/shard_map/ppermute | solution.py:428
  15.2 20.2 %collective-permute-start.6 = (bf16[192,768]{1,0:T(8,128)(2,1)S(1)}, bf16[192,768]{1,0:T(8,128)(2,1)S(1)}, u32[]{:S(2)}, u32[]{:S(2)}) collective-permute-start(bf16[192,768]{1,0:T(8,128)(2,1)S(1)} %collective-permute-done.2.refs_3_), channel_id=1, source_target_pairs={{0,2},{2,0},{4,6},{6,4},{8,10},{10,8},{12,14},{14,12},{1,3},{3,1},... | collective-permute-start | bytes 884744 | tf_op jit(solution)/shard_map/ppermute | solution.py:428
  32.8 9.9 %collective-permute-start.5 = (bf16[192,768]{1,0:T(8,128)(2,1)S(1)}, bf16[192,768]{1,0:T(8,128)(2,1)S(1)}, u32[]{:S(2)}, u32[]{:S(2)}) collective-permute-start(bf16[192,768]{1,0:T(8,128)(2,1)S(1)} %collective-permute-done.1.refs_2_), channel_id=1, source_target_pairs={{0,2},{2,0},{4,6},{6,4},{8,10},{10,8},{12,14},{14,12},{1,3},{3,1},... | collective-permute-start | bytes 884744 | tf_op jit(solution)/shard_map/ppermute | solution.py:428
  34.3 12.7 %collective-permute-start.4 = (bf16[192,768]{1,0:T(8,128)(2,1)S(1)}, bf16[192,768]{1,0:T(8,128)(2,1)S(1)}, u32[]{:S(2)}, u32[]{:S(2)}) collective-permute-start(bf16[192,768]{1,0:T(8,128)(2,1)S(1)} %collective-permute-done.refs_1_), channel_id=1, source_target_pairs={{0,2},{2,0},{4,6},{6,4},{8,10},{10,8},{12,14},{14,12},{1,3},{3,1},... | collective-permute-start | bytes 884744 | tf_op jit(solution)/shard_map/ppermute | solution.py:428
  61.3 10.0 %collective-permute-start.8 = (bf16[192,768]{1,0:T(8,128)(2,1)S(1)}, bf16[192,768]{1,0:T(8,128)(2,1)S(1)}, u32[]{:S(2)}, u32[]{:S(2)}) collective-permute-start(bf16[192,768]{1,0:T(8,128)(2,1)S(1)} %get-tuple-element.23), channel_id=1, source_target_pairs={{0,2},{2,0},{4,6},{6,4},{8,10},{10,8},{12,14},{14,12},{1,3},{3,1},... | collective-permute-start | bytes 884744 | tf_op jit(solution)/shard_map/ppermute | solution.py:428
  62.9 14.8 %collective-permute-start.10 = (bf16[192,768]{1,0:T(8,128)(2,1)S(1)}, bf16[192,768]{1,0:T(8,128)(2,1)S(1)}, u32[]{:S(2)}, u32[]{:S(2)}) collective-permute-start(bf16[192,768]{1,0:T(8,128)(2,1)S(1)} %get-tuple-element.25), channel_id=1, source_target_pairs={{0,2},{2,0},{4,6},{6,4},{8,10},{10,8},{12,14},{14,12},{1,3},{3,1},... | collective-permute-start | bytes 884744 | tf_op jit(solution)/shard_map/ppermute | solution.py:428
  63.4 24.9 %collective-permute-start.7 = (bf16[192,768]{1,0:T(8,128)(2,1)S(1)}, bf16[192,768]{1,0:T(8,128)(2,1)S(1)}, u32[]{:S(2)}, u32[]{:S(2)}) collective-permute-start(bf16[192,768]{1,0:T(8,128)(2,1)S(1)} %get-tuple-element.21), channel_id=1, source_target_pairs={{0,2},{2,0},{4,6},{6,4},{8,10},{10,8},{12,14},{14,12},{1,3},{3,1},... | collective-permute-start | bytes 884744 | tf_op jit(solution)/shard_map/ppermute | solution.py:428
  64.9 22.4 %collective-permute-start.12 = (bf16[192,768]{1,0:T(8,128)(2,1)S(1)}, bf16[192,768]{1,0:T(8,128)(2,1)S(1)}, u32[]{:S(2)}, u32[]{:S(2)}) collective-permute-start(bf16[192,768]{1,0:T(8,128)(2,1)S(1)} %get-tuple-element.27), channel_id=1, source_target_pairs={{0,2},{2,0},{4,6},{6,4},{8,10},{10,8},{12,14},{14,12},{1,3},{3,1},... | collective-permute-start | bytes 884744 | tf_op jit(solution)/shard_map/ppermute | solution.py:428
  71.4 16.9 %collective-permute-start.9 = (bf16[192,768]{1,0:T(8,128)(2,1)S(1)}, bf16[192,768]{1,0:T(8,128)(2,1)S(1)}, u32[]{:S(2)}, u32[]{:S(2)}) collective-permute-start(bf16[192,768]{1,0:T(8,128)(2,1)S(1)} %add_convert_fusion.2), channel_id=1, source_target_pairs={{0,8},{2,10},{4,12},{6,14},{8,0},{10,2},{12,4},{14,6},{1,9},{3,11}... | collective-permute-start | bytes 884744 | tf_op jit(solution)/shard_map/ppermute | solution.py:425
  77.7 10.6 %collective-permute-start.11 = (bf16[192,768]{1,0:T(8,128)(2,1)S(1)}, bf16[192,768]{1,0:T(8,128)(2,1)S(1)}, u32[]{:S(2)}, u32[]{:S(2)}) collective-permute-start(bf16[192,768]{1,0:T(8,128)(2,1)S(1)} %add_convert_fusion.1), channel_id=1, source_target_pairs={{0,12},{2,14},{4,0},{6,2},{8,4},{10,6},{12,8},{14,10},{1,13},{3,15... | collective-permute-start | bytes 884744 | tf_op jit(solution)/shard_map/ppermute | solution.py:425
  87.4 8.6 %collective-permute-start.13 = (bf16[192,768]{1,0:T(8,128)(2,1)S(1)}, bf16[192,768]{1,0:T(8,128)(2,1)S(1)}, u32[]{:S(2)}, u32[]{:S(2)}) collective-permute-start(bf16[192,768]{1,0:T(8,128)(2,1)S(1)} %add_convert_fusion), channel_id=1, source_target_pairs={{0,4},{2,6},{4,8},{6,10},{8,12},{10,14},{12,0},{14,2},{1,5},{3,7},... | collective-permute-start | bytes 884744 | tf_op jit(solution)/shard_map/ppermute | solution.py:425

commit v2 on v0

--- a/solution.py
+++ b/solution.py
@@ -3,6 +3,8 @@
 import jax
 import jax.numpy as jnp
 from jax import lax
+from jax.experimental import pallas as pl
+from jax.experimental.pallas import tpu as pltpu
 from jax.sharding import PartitionSpec as P
 
 HEAD_DIM = 64
@@ -80,7 +82,7 @@
     return (outputs, grad_query, local_dk, local_dv, global_dk, global_dv, local_ds, local_weight)
 
 
-def body(queries, key_input, value_input, grad_output, rand_blocks, global_pos):
+def sparse_body(queries, key_input, value_input, grad_output, rand_blocks, global_pos):
     tokens = queries.shape[0]
     blocks = tokens // BLOCK
     head_count = queries.shape[1] // HEAD_DIM
@@ -247,6 +249,203 @@
     return (rows_last(outputs), rows_last(grad_query), key_rows_out, value_rows_out)
 
 
+WHOLE_ROWS = 4096
+EXTRA = 16
+VMEM_BYTES = 48 * 1024 * 1024
+
+
+def dot(left, right, left_dim, right_dim):
+    return lax.dot_general(
+        left,
+        right,
+        (((left_dim,), (right_dim,)), ((), ())),
+        preferred_element_type=jnp.float32,
+    )
+
+
+def pack_kernel(rand_ref, key_ref, value_ref, query_ref, grad_ref, packed_ref):
+    tokens, width = key_ref.shape
+    heads = width // HEAD_DIM
+    blocks = tokens // BLOCK
+    lane = lax.broadcasted_iota(jnp.int32, (EXTRA, 2 * HEAD_DIM), 1)
+    for head in range(heads):
+        cols = slice(head * HEAD_DIM, (head + 1) * HEAD_DIM)
+        packed_ref[head, :tokens, : 2 * HEAD_DIM] = jnp.concatenate(
+            (key_ref[:, cols], value_ref[:, cols]), axis=1
+        )
+        packed_ref[head, :tokens, 2 * HEAD_DIM :] = jnp.concatenate(
+            (query_ref[:, cols], grad_ref[:, cols]), axis=1
+        )
+        listed = jnp.zeros((EXTRA, 2 * HEAD_DIM), jnp.int32)
+        for i in range(blocks * RAND):
+            entry = rand_ref[(i // RAND * heads + head) * RAND + i % RAND]
+            listed = jnp.where(lane == i, entry, listed)
+        listed = listed.astype(jnp.float32).astype(jnp.bfloat16)
+        packed_ref[head, tokens:, : 2 * HEAD_DIM] = listed
+        packed_ref[head, tokens:, 2 * HEAD_DIM :] = jnp.zeros_like(listed)
+    for slot in range(heads, packed_ref.shape[0]):
+        packed_ref[slot] = jnp.zeros(packed_ref.shape[1:], jnp.bfloat16)
+
+
+def unpack_kernel(packed_ref, attended_ref, query_ref, key_ref, value_ref):
+    heads = key_ref.shape[1] // HEAD_DIM
+    for head in range(heads):
+        cols = slice(head * HEAD_DIM, (head + 1) * HEAD_DIM)
+        for i, ref in enumerate((query_ref, attended_ref, key_ref, value_ref)):
+            ref[:, cols] = packed_ref[head, :, i * HEAD_DIM : (i + 1) * HEAD_DIM]
+
+
+def attend_kernel(
+    pos_row_ref, pos_col_ref, x_ref, out_ref, acc, global_kv, global_acc, listed, starts, sem
+):
+    shards, tokens, _ = out_ref.shape
+    stride = x_ref.shape[0] // shards
+    blocks = tokens // BLOCK
+    global_count = pos_row_ref.shape[1]
+    kv_cols = slice(0, 2 * HEAD_DIM)
+    rest_cols = slice(2 * HEAD_DIM, 4 * HEAD_DIM)
+
+    for shard in range(shards):
+        row = x_ref[shard * stride + tokens : (shard + 1) * stride, kv_cols].astype(jnp.float32)
+        passed = jnp.floor((row + 0.5) * (1.0 / blocks))
+        first = row * BLOCK + passed * (stride - tokens)
+        listed[shard] = first[:8].astype(jnp.int32)
+    copy = pltpu.make_async_copy(listed, starts, sem)
+    copy.start()
+    acc[...] = jnp.zeros_like(acc)
+    global_acc[...] = jnp.zeros_like(global_acc)
+    place = lax.broadcasted_iota(jnp.int32, (global_count, shards * stride), 1)
+    pick = (place == pos_col_ref[...]).astype(jnp.bfloat16)
+    global_kv[...] = dot(pick, x_ref[:, kv_cols], 1, 0).astype(jnp.bfloat16)
+    copy.wait()
+    lane = lax.broadcasted_iota(jnp.int32, (BLOCK, 6 * BLOCK), 1)
+    half = lax.broadcasted_iota(jnp.int32, (BLOCK, 2 * HEAD_DIM), 1) < HEAD_DIM
+    query_mask = jnp.where(half, 1.0 / math.sqrt(HEAD_DIM), 0.0).astype(jnp.bfloat16)
+    grad_mask = jnp.where(half, 0.0, 1.0).astype(jnp.bfloat16)
+
+    def at(start):
+        return pl.ds(pl.multiple_of(start, EXTRA), BLOCK)
+
+    def one_shard(shard, carry):
+        base = shard * stride
+        gkv = global_kv[...]
+        rows = []
+        for block in range(blocks):
+            rest = x_ref[at(base + block * BLOCK), rest_cols]
+            rows += [rest * query_mask, rest * grad_mask]
+        rows = jnp.concatenate(rows, axis=0)
+        global_dots = dot(rows, gkv, 1, 1)
+        before = jnp.maximum(shard - 1, 0) * stride + (blocks - 1) * BLOCK
+        after = jnp.minimum(shard + 1, shards - 1) * stride
+        global_sides = []
+        for block in range(blocks):
+            places = [
+                base + (block - 1) * BLOCK if block else before,
+                base + block * BLOCK,
+                base + (block + 1) * BLOCK if block < blocks - 1 else after,
+            ] + [starts[shard, 0, block * RAND + r] for r in range(RAND)]
+            places = [at(p) for p in places]
+            local_kv = jnp.concatenate([x_ref[p, kv_cols] for p in places], axis=0)
+            top = 2 * block * BLOCK
+            both = rows[top : top + 2 * BLOCK]
+            local_dots = dot(both, local_kv, 1, 1)
+            score, dp = local_dots[:BLOCK], local_dots[BLOCK:]
+            if block == 0:
+                score = jnp.where((lane < BLOCK) & (shard == 0), MASKED, score)
+            if block == blocks - 1:
+                outside = (lane >= 2 * BLOCK) & (lane < 3 * BLOCK)
+                score = jnp.where(outside & (shard == shards - 1), MASKED, score)
+            global_score = global_dots[top : top + BLOCK]
+            global_dp = global_dots[top + BLOCK : top + 2 * BLOCK]
+            highest = jnp.maximum(
+                jnp.max(score, axis=1, keepdims=True),
+                jnp.max(global_score, axis=1, keepdims=True),
+            )
+            local_exp = jnp.exp(score - highest)
+            global_exp = jnp.exp(global_score - highest)
+            inverse = 1.0 / (
+                jnp.sum(local_exp, axis=1, keepdims=True)
+                + jnp.sum(global_exp, axis=1, keepdims=True)
+            )
+            local_weight = (local_exp * inverse).astype(jnp.bfloat16)
+            global_weight = (global_exp * inverse).astype(jnp.bfloat16)
+            local_wf = local_weight.astype(jnp.float32)
+            global_wf = global_weight.astype(jnp.float32)
+            delta = jnp.sum(local_wf * dp, axis=1, keepdims=True) + jnp.sum(
+                global_wf * global_dp, axis=1, keepdims=True
+            )
+            local_ds = (local_wf * (dp - delta)).astype(jnp.bfloat16)
+            global_ds = (global_wf * (global_dp - delta)).astype(jnp.bfloat16)
+            local_side = jnp.concatenate((local_ds, local_weight), axis=0)
+            global_side = jnp.concatenate((global_ds, global_weight), axis=0)
+            global_sides.append(global_side)
+            result = dot(local_side, local_kv, 1, 0) + dot(global_side, gkv, 1, 0)
+            out_ref[shard, block * BLOCK : (block + 1) * BLOCK, kv_cols] = jnp.where(
+                half, result[:BLOCK] * (1.0 / math.sqrt(HEAD_DIM)), result[BLOCK:]
+            ).astype(jnp.bfloat16)
+            local_grad = dot(local_side, both, 0, 0)
+            for i, spot in enumerate(places):
+                acc[spot] += local_grad[i * BLOCK : (i + 1) * BLOCK]
+        global_acc[...] += dot(jnp.concatenate(global_sides, axis=0), rows, 0, 0)
+        return carry
+
+    lax.fori_loop(0, shards, one_shard, 0)
+    global_grad = global_acc[...].astype(jnp.bfloat16)
+    for shard in range(shards):
+        place = shard * stride + lax.broadcasted_iota(jnp.int32, (tokens, global_count), 0)
+        spread = (place == pos_row_ref[...]).astype(jnp.bfloat16)
+        out_ref[shard, :, rest_cols] = (
+            acc[shard * stride : shard * stride + tokens] + dot(spread, global_grad, 1, 0)
+        ).astype(jnp.bfloat16)
+
+
+def whole_body(queries, key_input, value_input, grad_output, rand_blocks, global_pos):
+    tokens, width = queries.shape
+    shards = lax.axis_size("seq")
+    global_count = global_pos.shape[0]
+    stride = tokens + EXTRA
+    pair = 2 * HEAD_DIM
+    bf16 = jnp.bfloat16
+    params = pltpu.CompilerParams(vmem_limit_bytes=VMEM_BYTES)
+    narrow = jax.ShapeDtypeStruct((tokens, width), bf16)
+    vmem = pl.BlockSpec(memory_space=pltpu.VMEM)
+    smem = pl.BlockSpec(memory_space=pltpu.SMEM)
+    packed = pl.pallas_call(
+        pack_kernel,
+        out_shape=jax.ShapeDtypeStruct((shards, stride, 2 * pair), bf16),
+        in_specs=[smem] + [vmem] * 4,
+        out_specs=vmem,
+        compiler_params=params,
+    )(rand_blocks.reshape(-1), key_input, value_input, queries, grad_output)
+    whole = lax.all_to_all(packed, "seq", split_axis=0, concat_axis=0, tiled=True)
+    place = global_pos + global_pos // tokens * EXTRA
+    result = pl.pallas_call(
+        attend_kernel,
+        out_shape=jax.ShapeDtypeStruct((shards, tokens, 2 * pair), bf16),
+        in_specs=[vmem] * 3,
+        out_specs=vmem,
+        scratch_shapes=[
+            pltpu.VMEM((shards * stride, pair), jnp.float32),
+            pltpu.VMEM((global_count, pair), bf16),
+            pltpu.VMEM((global_count, pair), jnp.float32),
+            pltpu.VMEM((shards, 8, pair), jnp.int32),
+            pltpu.SMEM((shards, 8, pair), jnp.int32),
+            pltpu.SemaphoreType.DMA,
+        ],
+        compiler_params=params,
+    )(place.reshape(1, -1), place.reshape(-1, 1), whole.reshape(shards * stride, 2 * pair))
+    returned = lax.all_to_all(result, "seq", split_axis=0, concat_axis=0, tiled=True)
+    return pl.pallas_call(unpack_kernel, out_shape=(narrow,) * 4, compiler_params=params)(returned)
+
+
+def body(queries, *others):
+    shards = lax.axis_size("seq")
+    tokens, width = queries.shape
+    if width // HEAD_DIM <= shards and shards * tokens <= WHOLE_ROWS:
+        return whole_body(queries, *others)
+    return sparse_body(queries, *others)
+
+
 def solution(mesh):
     in_specs = (
         P(("groups", "seq"), "head"),

time: 265 us -> 77.4 us (0.29)
  waiting for transfers between devices: 67.8 us -> 21.5 us
  matrix products: 38 us -> 0 us
  local copies, waits for them, and re-layouts: 40.9 us -> 4.65 us
  blocking collectives: 48.3 us -> 23.6 us
  other arithmetic: 24.2 us -> 0.01 us
  starting transfers between devices: 29.4 us -> 7.38 us
  Pallas kernels: 0 us -> 19.2 us
  between operations: 14.7 us -> 0.67 us
    psum x1 -> x0, waiting for transfers between devices: 66.3 us -> none  [body(): global_total = lax.psum(global_grad, 'seq')]
    psum x1 -> x0, blocking collectives: 48.3 us -> none  [body(): global_kv = lax.psum(partial_rows, 'seq').astype(jnp.bfloat16)]
    dot_general x74 -> x0, matrix products: 38 us -> none  [the longest x6 5.75 us: attend_head(): jnp.einsum('nqk,nqe->nke', local_ds, query, preferred_element_type=jnp.fl...]
    all_to_all x0 -> x1, blocking collectives: none -> 23.6 us  [whole_body(): lax.all_to_all(result, 'seq', split_axis=0, concat_axis=0, tiled=True)]
    all_to_all x3 -> x1, waiting for transfers between devices: 0.01 us -> 21.5 us  [whole_body(): lax.all_to_all(packed, 'seq', split_axis=0, concat_axis=0, tiled=True)]
    pallas_call x0 -> x3, Pallas kernels: none -> 19.2 us  [the longest x1 16.5 us: whole_body(): pl.pallas_call(attend_kernel, out_shape=jax.ShapeDtypeStruct((shards, tok...]
    all_to_all x3 -> x1, starting transfers between devices: 18.9 us -> 7.38 us  [whole_body(): lax.all_to_all(packed, 'seq', split_axis=0, concat_axis=0, tiled=True)]
    ppermute x4 -> x0, starting transfers between devices: 10.5 us -> none  [the longest x2 7.69 us: with_halo(): before = lax.ppermute(last, axis, up)]
  transfers between devices with their start and end apart: 8 -> 1, of which waited for: 2 -> 1; matrix products, arithmetic and copies ran while one was open for 11% -> 0% of each run, Pallas kernels for 0% -> 0%
where the time goes in v2:
time: 77.4 us; the launch traced here: 77 us
  blocking collectives  23.6 us (30%)
  waiting for transfers between devices  21.5 us (28%)
  Pallas kernels  19.2 us (25%)
  starting transfers between devices  7.38 us (10%)
  local copies, waits for them, and re-layouts  4.65 us (6%)
    all_to_all x1, blocking collectives, whole_body(): lax.all_to_all(result, 'seq', split_axis=0, concat_axis=0, tiled=True)  23.6 us
    all_to_all x1, waiting for transfers between devices, whole_body(): lax.all_to_all(packed, 'seq', split_axis=0, concat_axis=0, tiled=True)  21.5 us
    pallas_call x1, Pallas kernels, whole_body(): pl.pallas_call(attend_kernel, out_shape=jax.ShapeDtypeStruct((shards, tok...  16.5 us
    all_to_all x1, starting transfers between devices, whole_body(): lax.all_to_all(packed, 'seq', split_axis=0, concat_axis=0, tiled=True)  7.38 us
    unnamed x11, local copies, waits for them, and re-layouts  4.43 us
    pallas_call x1, Pallas kernels, whole_body(): pl.pallas_call(pack_kernel, out_shape=jax.ShapeDtypeStruct((shards, strid...  1.66 us
  transfers between devices with their start and end apart: 1, of which 1 were waited for; matrix products, arithmetic and copies ran while one was open for 0% of the time, Pallas kernels for 0%

profile of v2, /device:TPU:0, one launch (start us, length us, event | category | flops | bytes accessed | tf_op | source)
XLA Modules:
  0.0 77.0 jit_solution(12461699605381158933)
XLA Ops:
  0.6 0.8 %copy.11 = s32[3,6,3]{2,1,0:T(8,128)S(1)} copy(s32[3,6,3]{1,2,0:T(4,128)} %param.10) | data formatting | bytes 432 | tf_op args[4]
  1.4 0.1 reshape.22.rand_ref
  1.5 0.0 copy-start
  1.5 0.9 %copy-done = bf16[192,384]{1,0:T(8,128)(2,1)S(1)} copy-done((bf16[192,384]{1,0:T(8,128)(2,1)S(1)}, bf16[192,384]{1,0:T(8,128)(2,1)}, u32[]{:S(2)}) %copy-start) | copy-done | bytes 147480
  2.4 0.0 copy-start.1
  2.4 0.9 %copy-done.1 = bf16[192,384]{1,0:T(8,128)(2,1)S(1)} copy-done((bf16[192,384]{1,0:T(8,128)(2,1)S(1)}, bf16[192,384]{1,0:T(8,128)(2,1)}, u32[]{:S(2)}) %copy-start.1) | copy-done | bytes 147480
  3.3 0.0 copy-start.2
  3.3 0.9 %copy-done.2 = bf16[192,384]{1,0:T(8,128)(2,1)S(1)} copy-done((bf16[192,384]{1,0:T(8,128)(2,1)S(1)}, bf16[192,384]{1,0:T(8,128)(2,1)}, u32[]{:S(2)}) %copy-start.2) | copy-done | bytes 147480
  4.2 0.0 copy-start.3
  4.2 0.9 %copy-done.3 = bf16[192,384]{1,0:T(8,128)(2,1)S(1)} copy-done((bf16[192,384]{1,0:T(8,128)(2,1)S(1)}, bf16[192,384]{1,0:T(8,128)(2,1)}, u32[]{:S(2)}) %copy-start.3) | copy-done | bytes 147480
  5.2 1.7 %shard_map.93 = bf16[8,208,256]{2,1,0:T(8,128)(2,1)} custom-call(s32[54]{0:T(128)S(1)} %reshape.22.rand_ref, bf16[192,384]{1,0:T(8,128)(2,1)S(1)} %copy-done, bf16[192,384]{1,0:T(8,128)(2,1)S(1)} %copy-done.1, bf16[192,384]{1,0:T(8,128)(2,1)S(1)} %copy-done.2, bf16[192,384]{1,0:T(8,128)(2,1)S(1)} %copy-done.3), custom_call_target="tpu_custom_call" | custom-call | tf_op jit(solution)/shard_map/pallas_call | solution.py:413
  6.8 0.0 copy-start.4
  6.8 7.4 %all-to-all-start = ((bf16[8,208,256]{2,1,0:T(8,128)(2,1)}), bf16[8,208,256]{2,1,0:T(8,128)(2,1)S(1)}, u32[]{:S(2)}, u32[]{:S(2)}) async-start(bf16[8,208,256]{2,1,0:T(8,128)(2,1)} %shard_map.93), calls=%async_computation | async-start | bytes 1703936 | tf_op jit(solution)/shard_map/all_to_all | solution.py:420
  14.2 0.0 copy-done.4
  14.2 0.1 copy.12.pos_col_ref
  14.4 21.5 %all-to-all-done = bf16[8,208,256]{2,1,0:T(8,128)(2,1)S(1)} async-done(((bf16[8,208,256]{2,1,0:T(8,128)(2,1)}), bf16[8,208,256]{2,1,0:T(8,128)(2,1)S(1)}, u32[]{:S(2)}, u32[]{:S(2)}) %all-to-all-start) | async-done | bytes 852000 | tf_op jit(solution)/shard_map/all_to_all | solution.py:420
  35.8 16.5 %shard_map.94 = bf16[8,192,256]{2,1,0:T(8,128)(2,1)S(1)} custom-call(s32[1,256]{1,0:T(1,128)S(1)} %bitcast.5, s32[256,1]{1,0:T(8,128)S(1)} %copy.12.pos_col_ref, bf16[1664,256]{1,0:T(8,128)(2,1)S(1)} %bitcast.3), custom_call_target="tpu_custom_call" | custom-call | tf_op jit(solution)/shard_map/pallas_call | solution.py:422
  52.3 23.6 %all_to_all.10.packed_ref = bf16[8,192,256]{2,1,0:T(8,128)(2,1)S(1)} all-to-all(bf16[8,192,256]{2,1,0:T(8,128)(2,1)S(1)} %shard_map.94), channel_id=1, replica_groups=mesh['groups'=2,'seq'=8,'head'=2] {'seq'}, dimensions={0} | all-to-all | bytes 1572864 | tf_op jit(solution)/shard_map/all_to_all | solution.py:437
  75.9 1.1 %shard_map.95 = (bf16[192,384]{1,0:T(8,128)(2,1)}, bf16[192,384]{1,0:T(8,128)(2,1)}, bf16[192,384]{1,0:T(8,128)(2,1)}, bf16[192,384]{1,0:T(8,128)(2,1)}) custom-call(bf16[8,192,256]{2,1,0:T(8,128)(2,1)S(1)} %all_to_all.10.packed_ref), custom_call_target="tpu_custom_call" | custom-call | tf_op jit(solution)/shard_map/pallas_call | solution.py:438
  (1 shorter events, 0.0 us)
Async XLA Ops:
  1.5 0.9 %copy-start = (bf16[192,384]{1,0:T(8,128)(2,1)S(1)}, bf16[192,384]{1,0:T(8,128)(2,1)}, u32[]{:S(2)}) copy-start(bf16[192,384]{1,0:T(8,128)(2,1)} %key_ref.1) | copy-start | bytes 442372
  2.4 0.9 %copy-start.1 = (bf16[192,384]{1,0:T(8,128)(2,1)S(1)}, bf16[192,384]{1,0:T(8,128)(2,1)}, u32[]{:S(2)}) copy-start(bf16[192,384]{1,0:T(8,128)(2,1)} %value_ref.1) | copy-start | bytes 442372
  3.3 0.9 %copy-start.2 = (bf16[192,384]{1,0:T(8,128)(2,1)S(1)}, bf16[192,384]{1,0:T(8,128)(2,1)}, u32[]{:S(2)}) copy-start(bf16[192,384]{1,0:T(8,128)(2,1)} %query_ref.1) | copy-start | bytes 442372
  4.2 0.9 %copy-start.3 = (bf16[192,384]{1,0:T(8,128)(2,1)S(1)}, bf16[192,384]{1,0:T(8,128)(2,1)}, u32[]{:S(2)}) copy-start(bf16[192,384]{1,0:T(8,128)(2,1)} %grad_ref.1) | copy-start | bytes 442372
  6.8 7.4 %copy-start.4 = (s32[256]{0:T(256)S(1)}, s32[256]{0:T(256)}, u32[]{:S(2)}) copy-start(s32[256]{0:T(256)} %param.11) | copy-start | bytes 3076
  6.8 29.0 %all-to-all-start = ((bf16[8,208,256]{2,1,0:T(8,128)(2,1)}), bf16[8,208,256]{2,1,0:T(8,128)(2,1)S(1)}, u32[]{:S(2)}, u32[]{:S(2)}) async-start(bf16[8,208,256]{2,1,0:T(8,128)(2,1)} %shard_map.93), calls=%async_computation | async-start | bytes 1703936 | tf_op jit(solution)/shard_map/all_to_all | solution.py:420

commit v3 on v0

--- a/solution.py
+++ b/solution.py
@@ -3,6 +3,8 @@
 import jax
 import jax.numpy as jnp
 from jax import lax
+from jax.experimental import pallas as pl
+from jax.experimental.pallas import tpu as pltpu
 from jax.sharding import PartitionSpec as P
 
 HEAD_DIM = 64
@@ -80,7 +82,7 @@
     return (outputs, grad_query, local_dk, local_dv, global_dk, global_dv, local_ds, local_weight)
 
 
-def body(queries, key_input, value_input, grad_output, rand_blocks, global_pos):
+def sparse_body(queries, key_input, value_input, grad_output, rand_blocks, global_pos):
     tokens = queries.shape[0]
     blocks = tokens // BLOCK
     head_count = queries.shape[1] // HEAD_DIM
@@ -247,6 +249,253 @@
     return (rows_last(outputs), rows_last(grad_query), key_rows_out, value_rows_out)
 
 
+WHOLE_ROWS = 4096
+GROUP = 4
+VMEM_BYTES = 32 * 1024 * 1024
+
+
+def dot(left, right, left_dim, right_dim):
+    return lax.dot_general(
+        left,
+        right,
+        (((left_dim,), (right_dim,)), ((), ())),
+        preferred_element_type=jnp.float32,
+    )
+
+
+def listed_rows(tokens):
+    return -(-(tokens // BLOCK * RAND) // 16) * 16
+
+
+def pack_kernel(rand_hbm, key_hbm, value_hbm, query_hbm, grad_hbm, packed_ref, *scratch):
+    *targets, listed, sems = scratch
+    _, key_ref, value_ref, query_ref, grad_ref = targets
+    tokens, width = key_ref.shape
+    heads = width // HEAD_DIM
+    copies = [
+        pltpu.make_async_copy(source, target, sems.at[i])
+        for i, (source, target) in enumerate(
+            zip((rand_hbm, key_hbm, value_hbm, query_hbm, grad_hbm), targets)
+        )
+    ]
+    for copy in copies:
+        copy.start()
+    listed[...] = jnp.zeros_like(listed)
+    for slot in range(heads, packed_ref.shape[0]):
+        packed_ref[slot] = jnp.zeros(packed_ref.shape[1:], jnp.bfloat16)
+    for copy in copies:
+        copy.wait()
+    for block in range(tokens // BLOCK):
+        listed[block * RAND : (block + 1) * RAND, :heads] = targets[0][block]
+    entries = listed[...].astype(jnp.float32).astype(jnp.bfloat16)
+    for head in range(heads):
+        cols = slice(head * HEAD_DIM, (head + 1) * HEAD_DIM)
+        packed_ref[head, :tokens, : 2 * HEAD_DIM] = jnp.concatenate(
+            (key_ref[:, cols], value_ref[:, cols]), axis=1
+        )
+        packed_ref[head, :tokens, 2 * HEAD_DIM :] = jnp.concatenate(
+            (query_ref[:, cols], grad_ref[:, cols]), axis=1
+        )
+        packed_ref[head, tokens:, : 2 * HEAD_DIM] = entries
+        packed_ref[head, tokens:, 2 * HEAD_DIM :] = jnp.zeros_like(entries)
+
+
+def unpack_kernel(packed_ref, attended_ref, query_ref, key_ref, value_ref):
+    heads = key_ref.shape[1] // HEAD_DIM
+    for head in range(heads):
+        cols = slice(head * HEAD_DIM, (head + 1) * HEAD_DIM)
+        for i, ref in enumerate((query_ref, attended_ref, key_ref, value_ref)):
+            ref[:, cols] = packed_ref[head, :, i * HEAD_DIM : (i + 1) * HEAD_DIM]
+
+
+def attend_kernel(
+    pos_row_ref, pos_col_ref, x_ref, out_ref, acc, global_kv, global_acc, listed, starts, sem
+):
+    shards, tokens, _ = out_ref.shape
+    stride = x_ref.shape[0] // shards
+    blocks = tokens // BLOCK
+    global_count = pos_row_ref.shape[1]
+    own = lax.axis_index("seq")
+    kv_cols = slice(0, 2 * HEAD_DIM)
+    rest_cols = slice(2 * HEAD_DIM, 4 * HEAD_DIM)
+
+    for shard in range(shards):
+        row = x_ref[shard * stride + tokens : (shard + 1) * stride, kv_cols].astype(jnp.float32)
+        passed = jnp.floor((row + 0.5) * (1.0 / blocks))
+        first = row * BLOCK + passed * (stride - tokens)
+        listed[shard] = first.astype(jnp.int32)
+    copy = pltpu.make_async_copy(listed, starts, sem)
+    copy.start()
+    acc[...] = jnp.zeros_like(acc)
+    global_acc[...] = jnp.zeros_like(global_acc)
+    place = lax.broadcasted_iota(jnp.int32, (global_count, shards * stride), 1)
+    pick = (place == pos_col_ref[...]).astype(jnp.bfloat16)
+    global_kv[...] = dot(pick, x_ref[:, kv_cols], 1, 0).astype(jnp.bfloat16)
+    copy.wait()
+    lane = lax.broadcasted_iota(jnp.int32, (BLOCK, 6 * BLOCK), 1)
+    half = lax.broadcasted_iota(jnp.int32, (BLOCK, 2 * HEAD_DIM), 1) < HEAD_DIM
+    query_mask = jnp.where(half, 1.0 / math.sqrt(HEAD_DIM), 0.0).astype(jnp.bfloat16)
+    grad_mask = jnp.where(half, 0.0, 1.0).astype(jnp.bfloat16)
+
+    def at(start):
+        return pl.ds(pl.multiple_of(start, 16), BLOCK)
+
+    def products(shard):
+        base = shard * stride
+        before = jnp.maximum(shard - 1, 0) * stride + (blocks - 1) * BLOCK
+        after = jnp.minimum(shard + 1, shards - 1) * stride
+        rows = []
+        for block in range(blocks):
+            rest = x_ref[at(base + block * BLOCK), rest_cols]
+            rows += [rest * query_mask, rest * grad_mask]
+        rows = jnp.concatenate(rows, axis=0)
+        all_places, local_kvs, local_dots = [], [], []
+        for block in range(blocks):
+            places = [
+                base + (block - 1) * BLOCK if block else before,
+                base + block * BLOCK,
+                base + (block + 1) * BLOCK if block < blocks - 1 else after,
+            ] + [starts[shard, block * RAND + r, own] for r in range(RAND)]
+            all_places.append([at(p) for p in places])
+            local_kvs.append(jnp.concatenate([x_ref[p, kv_cols] for p in all_places[-1]], axis=0))
+            both = rows[2 * block * BLOCK : 2 * (block + 1) * BLOCK]
+            local_dots.append(dot(both, local_kvs[-1], 1, 1))
+        return rows, all_places, local_kvs, local_dots, dot(rows, global_kv[...], 1, 1)
+
+    def weigh(shard, block, local_dots, global_dots):
+        score, dp = local_dots[:BLOCK], local_dots[BLOCK:]
+        if block == 0:
+            score = jnp.where((lane < BLOCK) & (shard == 0), MASKED, score)
+        if block == blocks - 1:
+            outside = (lane >= 2 * BLOCK) & (lane < 3 * BLOCK)
+            score = jnp.where(outside & (shard == shards - 1), MASKED, score)
+        global_score, global_dp = global_dots[:BLOCK], global_dots[BLOCK:]
+        highest = jnp.maximum(
+            jnp.max(score, axis=1, keepdims=True),
+            jnp.max(global_score, axis=1, keepdims=True),
+        )
+        local_exp = jnp.exp(score - highest)
+        global_exp = jnp.exp(global_score - highest)
+        inverse = 1.0 / (
+            jnp.sum(local_exp, axis=1, keepdims=True)
+            + jnp.sum(global_exp, axis=1, keepdims=True)
+        )
+        local_weight = (local_exp * inverse).astype(jnp.bfloat16)
+        global_weight = (global_exp * inverse).astype(jnp.bfloat16)
+        local_wf = local_weight.astype(jnp.float32)
+        global_wf = global_weight.astype(jnp.float32)
+        delta = jnp.sum(local_wf * dp, axis=1, keepdims=True) + jnp.sum(
+            global_wf * global_dp, axis=1, keepdims=True
+        )
+        local_ds = (local_wf * (dp - delta)).astype(jnp.bfloat16)
+        global_ds = (global_wf * (global_dp - delta)).astype(jnp.bfloat16)
+        return (
+            jnp.concatenate((local_ds, local_weight), axis=0),
+            jnp.concatenate((global_ds, global_weight), axis=0),
+        )
+
+    def shard_group(group, carry):
+        members = [group * GROUP + i for i in range(GROUP)]
+        made = [products(shard) for shard in members]
+        sides = [
+            [
+                weigh(
+                    shard,
+                    block,
+                    local_dots[block],
+                    global_dots[2 * block * BLOCK : 2 * (block + 1) * BLOCK],
+                )
+                for block in range(blocks)
+            ]
+            for shard, (_, _, _, local_dots, global_dots) in zip(members, made)
+        ]
+        gkv = global_kv[...]
+        for shard, side, (rows, all_places, local_kvs, _, _) in zip(members, sides, made):
+            global_side = jnp.concatenate([pair[1] for pair in side], axis=0)
+            global_result = dot(global_side, gkv, 1, 0)
+            results, grads = [], []
+            for block in range(blocks):
+                span = slice(2 * block * BLOCK, 2 * (block + 1) * BLOCK)
+                results.append(dot(side[block][0], local_kvs[block], 1, 0) + global_result[span])
+                grads.append(dot(side[block][0], rows[span], 0, 0))
+            global_acc[...] += dot(global_side, rows, 0, 0)
+            for block in range(blocks):
+                out_ref[shard, block * BLOCK : (block + 1) * BLOCK, kv_cols] = jnp.where(
+                    half,
+                    results[block][:BLOCK] * (1.0 / math.sqrt(HEAD_DIM)),
+                    results[block][BLOCK:],
+                ).astype(jnp.bfloat16)
+                for i, spot in enumerate(all_places[block]):
+                    acc[spot] += grads[block][i * BLOCK : (i + 1) * BLOCK]
+        return carry
+
+    lax.fori_loop(0, shards // GROUP, shard_group, 0)
+    global_grad = global_acc[...].astype(jnp.bfloat16)
+    for shard in range(shards):
+        place = shard * stride + lax.broadcasted_iota(jnp.int32, (tokens, global_count), 0)
+        spread = (place == pos_row_ref[...]).astype(jnp.bfloat16)
+        out_ref[shard, :, rest_cols] = (
+            acc[shard * stride : shard * stride + tokens] + dot(spread, global_grad, 1, 0)
+        ).astype(jnp.bfloat16)
+
+
+def attend(whole, place):
+    shards, stride, _ = whole.shape
+    tokens = stride - listed_rows(stride - stride % BLOCK)
+    extra = stride - tokens
+    pair = 2 * HEAD_DIM
+    global_count = place.shape[0]
+    return pl.pallas_call(
+        attend_kernel,
+        out_shape=jax.ShapeDtypeStruct((shards, tokens, 2 * pair), jnp.bfloat16),
+        scratch_shapes=[
+            pltpu.VMEM((shards * stride, pair), jnp.float32),
+            pltpu.VMEM((global_count, pair), jnp.bfloat16),
+            pltpu.VMEM((global_count, pair), jnp.float32),
+            pltpu.VMEM((shards, extra, pair), jnp.int32),
+            pltpu.SMEM((shards, extra, pair), jnp.int32),
+            pltpu.SemaphoreType.DMA,
+        ],
+        compiler_params=pltpu.CompilerParams(vmem_limit_bytes=VMEM_BYTES),
+    )(place.reshape(1, -1), place.reshape(-1, 1), whole.reshape(shards * stride, 2 * pair))
+
+
+def whole_body(queries, key_input, value_input, grad_output, rand_blocks, global_pos):
+    tokens, width = queries.shape
+    shards = lax.axis_size("seq")
+    extra = listed_rows(tokens)
+    stride = tokens + extra
+    narrow = jax.ShapeDtypeStruct((tokens, width), jnp.bfloat16)
+    rand_lists = rand_blocks.transpose(0, 2, 1)
+    packed = pl.pallas_call(
+        pack_kernel,
+        out_shape=jax.ShapeDtypeStruct((shards, stride, 4 * HEAD_DIM), jnp.bfloat16),
+        in_specs=[pl.BlockSpec(memory_space=pl.ANY)] * 5,
+        scratch_shapes=[pltpu.VMEM(rand_lists.shape, jnp.int32)]
+        + [pltpu.VMEM((tokens, width), jnp.bfloat16)] * 4
+        + [
+            pltpu.VMEM((extra, 2 * HEAD_DIM), jnp.int32),
+            pltpu.SemaphoreType.DMA((5,)),
+        ],
+    )(rand_lists, key_input, value_input, queries, grad_output)
+    whole = lax.all_to_all(packed, "seq", split_axis=0, concat_axis=0, tiled=True)
+    result = attend(whole, global_pos + global_pos // tokens * extra)
+    returned = lax.all_to_all(result, "seq", split_axis=0, concat_axis=0, tiled=True)
+    return pl.pallas_call(
+        unpack_kernel,
+        out_shape=(narrow,) * 4,
+        compiler_params=pltpu.CompilerParams(vmem_limit_bytes=VMEM_BYTES),
+    )(returned)
+
+
+def body(queries, *others):
+    shards = lax.axis_size("seq")
+    tokens, width = queries.shape
+    if width // HEAD_DIM <= shards and shards * tokens <= WHOLE_ROWS:
+        return whole_body(queries, *others)
+    return sparse_body(queries, *others)
+
+
 def solution(mesh):
     in_specs = (
         P(("groups", "seq"), "head"),

time: 265 us -> 64.3 us (0.24)
  waiting for transfers between devices: 67.8 us -> 21.5 us
  local copies, waits for them, and re-layouts: 40.9 us -> 0.14 us
  matrix products: 38 us -> 0 us
  blocking collectives: 48.3 us -> 23.6 us
  other arithmetic: 24.2 us -> 0.01 us
  starting transfers between devices: 29.4 us -> 7.26 us
  between operations: 14.7 us -> 0.67 us
  Pallas kernels: 0 us -> 10.9 us
    psum x1 -> x0, waiting for transfers between devices: 66.3 us -> none  [body(): global_total = lax.psum(global_grad, 'seq')]
    psum x1 -> x0, blocking collectives: 48.3 us -> none  [body(): global_kv = lax.psum(partial_rows, 'seq').astype(jnp.bfloat16)]
    dot_general x74 -> x0, matrix products: 38 us -> none  [the longest x6 5.75 us: attend_head(): jnp.einsum('nqk,nqe->nke', local_ds, query, preferred_element_type=jnp.fl...]
    all_to_all x0 -> x1, blocking collectives: none -> 23.6 us  [whole_body(): lax.all_to_all(result, 'seq', split_axis=0, concat_axis=0, tiled=True)]
    all_to_all x3 -> x1, waiting for transfers between devices: 0.01 us -> 21.5 us  [whole_body(): lax.all_to_all(packed, 'seq', split_axis=0, concat_axis=0, tiled=True)]
    all_to_all x3 -> x1, starting transfers between devices: 18.9 us -> 7.26 us  [whole_body(): lax.all_to_all(packed, 'seq', split_axis=0, concat_axis=0, tiled=True)]
    pallas_call x0 -> x3, Pallas kernels: none -> 10.9 us  [the longest x1 7.53 us: attend(): pl.pallas_call(attend_kernel, out_shape=jax.ShapeDtypeStruct((shards, tok...]
    ppermute x4 -> x0, starting transfers between devices: 10.5 us -> none  [the longest x2 7.69 us: with_halo(): before = lax.ppermute(last, axis, up)]
  transfers between devices with their start and end apart: 8 -> 1, of which waited for: 2 -> 1; matrix products, arithmetic and copies ran while one was open for 11% -> 0% of each run, Pallas kernels for 0% -> 0%
where the time goes in v3:
time: 64.3 us; the launch traced here: 64.1 us
  blocking collectives  23.6 us (37%)
  waiting for transfers between devices  21.5 us (33%)
  Pallas kernels  10.9 us (17%)
  starting transfers between devices  7.26 us (11%)
  between operations  0.67 us (1%)
    all_to_all x1, blocking collectives, whole_body(): lax.all_to_all(result, 'seq', split_axis=0, concat_axis=0, tiled=True)  23.6 us
    all_to_all x1, waiting for transfers between devices, whole_body(): lax.all_to_all(packed, 'seq', split_axis=0, concat_axis=0, tiled=True)  21.5 us
    pallas_call x1, Pallas kernels, attend(): pl.pallas_call(attend_kernel, out_shape=jax.ShapeDtypeStruct((shards, tok...  7.53 us
    all_to_all x1, starting transfers between devices, whole_body(): lax.all_to_all(packed, 'seq', split_axis=0, concat_axis=0, tiled=True)  7.26 us
    pallas_call x1, Pallas kernels, whole_body(): pl.pallas_call(pack_kernel, out_shape=jax.ShapeDtypeStruct((shards, strid...  2.31 us
  transfers between devices with their start and end apart: 1, of which 1 were waited for; matrix products, arithmetic and copies ran while one was open for 0% of the time, Pallas kernels for 0%

profile of v3, /device:TPU:0, one launch (start us, length us, event | category | flops | bytes accessed | tf_op | source)
XLA Modules:
  0.0 64.1 jit_solution(16915209245289917573)
XLA Ops:
  0.6 2.3 %shard_map.93 = bf16[8,208,256]{2,1,0:T(8,128)(2,1)} custom-call(s32[3,3,6]{2,1,0:T(4,128)} %bitcast.7, bf16[192,384]{1,0:T(8,128)(2,1)} %key_hbm.1, bf16[192,384]{1,0:T(8,128)(2,1)} %value_hbm.1, bf16[192,384]{1,0:T(8,128)(2,1)} %query_hbm.1, bf16[192,384]{1,0:T(8,128)(2,1)} %grad_hbm.1), custom_call_target="tpu_custom_call" | custom-call | tf_op jit(solution)/shard_map/pallas_call | solution.py:470
  3.0 0.0 copy-start
  3.0 7.3 %all-to-all-start = ((bf16[8,208,256]{2,1,0:T(8,128)(2,1)}), bf16[8,208,256]{2,1,0:T(8,128)(2,1)S(1)}, u32[]{:S(2)}, u32[]{:S(2)}) async-start(bf16[8,208,256]{2,1,0:T(8,128)(2,1)} %shard_map.93), calls=%async_computation | async-start | bytes 1703936 | tf_op jit(solution)/shard_map/all_to_all | solution.py:481
  10.2 0.0 copy-done
  10.3 0.1 copy.10.pos_col_ref
  10.4 21.5 %all-to-all-done = bf16[8,208,256]{2,1,0:T(8,128)(2,1)S(1)} async-done(((bf16[8,208,256]{2,1,0:T(8,128)(2,1)}), bf16[8,208,256]{2,1,0:T(8,128)(2,1)S(1)}, u32[]{:S(2)}, u32[]{:S(2)}) %all-to-all-start) | async-done | bytes 852000 | tf_op jit(solution)/shard_map/all_to_all | solution.py:481
  31.9 7.5 %shard_map.94 = bf16[8,192,256]{2,1,0:T(8,128)(2,1)S(1)} custom-call(s32[1,256]{1,0:T(1,128)S(1)} %bitcast.6, s32[256,1]{1,0:T(8,128)S(1)} %copy.10.pos_col_ref, bf16[1664,256]{1,0:T(8,128)(2,1)S(1)} %bitcast.4), custom_call_target="tpu_custom_call" | custom-call | tf_op jit(solution)/shard_map/pallas_call | solution.py:448
  39.4 23.6 %all_to_all.10.packed_ref = bf16[8,192,256]{2,1,0:T(8,128)(2,1)S(1)} all-to-all(bf16[8,192,256]{2,1,0:T(8,128)(2,1)S(1)} %shard_map.94), channel_id=1, replica_groups=mesh['groups'=2,'seq'=8,'head'=2] {'seq'}, dimensions={0} | all-to-all | bytes 1572864 | tf_op jit(solution)/shard_map/all_to_all | solution.py:483
  62.9 1.1 %shard_map.95 = (bf16[192,384]{1,0:T(8,128)(2,1)}, bf16[192,384]{1,0:T(8,128)(2,1)}, bf16[192,384]{1,0:T(8,128)(2,1)}, bf16[192,384]{1,0:T(8,128)(2,1)}) custom-call(bf16[8,192,256]{2,1,0:T(8,128)(2,1)S(1)} %all_to_all.10.packed_ref), custom_call_target="tpu_custom_call" | custom-call | tf_op jit(solution)/shard_map/pallas_call | solution.py:484
  (1 shorter events, 0.0 us)
Async XLA Ops:
  3.0 7.3 %copy-start = (s32[256]{0:T(256)S(1)}, s32[256]{0:T(256)}, u32[]{:S(2)}) copy-start(s32[256]{0:T(256)} %param.11) | copy-start | bytes 3076
  3.0 28.9 %all-to-all-start = ((bf16[8,208,256]{2,1,0:T(8,128)(2,1)}), bf16[8,208,256]{2,1,0:T(8,128)(2,1)S(1)}, u32[]{:S(2)}, u32[]{:S(2)}) async-start(bf16[8,208,256]{2,1,0:T(8,128)(2,1)} %shard_map.93), calls=%async_computation | async-start | bytes 1703936 | tf_op jit(solution)/shard_map/all_to_all | solution.py:481

commit v4 on v3

--- a/solution.py
+++ b/solution.py
@@ -267,70 +267,87 @@
     return -(-(tokens // BLOCK * RAND) // 16) * 16
 
 
-def pack_kernel(rand_hbm, key_hbm, value_hbm, query_hbm, grad_hbm, packed_ref, *scratch):
-    *targets, listed, sems = scratch
-    _, key_ref, value_ref, query_ref, grad_ref = targets
+def pack_kernel(rand_hbm, key_hbm, value_hbm, query_hbm, grad_hbm, packed_hbm, *scratch):
+    *targets, listed, packed, sems, out_sems = scratch
+    rand_ref, key_ref, value_ref, query_ref, grad_ref = targets
     tokens, width = key_ref.shape
     heads = width // HEAD_DIM
+    slots = packed.shape[0]
     copies = [
         pltpu.make_async_copy(source, target, sems.at[i])
         for i, (source, target) in enumerate(
             zip((rand_hbm, key_hbm, value_hbm, query_hbm, grad_hbm), targets)
         )
     ]
+    sends = [
+        pltpu.make_async_copy(packed.at[slot], packed_hbm.at[slot], out_sems.at[slot])
+        for slot in range(slots)
+    ]
     for copy in copies:
         copy.start()
     listed[...] = jnp.zeros_like(listed)
-    for slot in range(heads, packed_ref.shape[0]):
-        packed_ref[slot] = jnp.zeros(packed_ref.shape[1:], jnp.bfloat16)
+    for slot in range(heads, slots):
+        packed[slot] = jnp.zeros(packed.shape[1:], jnp.bfloat16)
+        sends[slot].start()
     for copy in copies:
         copy.wait()
     for block in range(tokens // BLOCK):
-        listed[block * RAND : (block + 1) * RAND, :heads] = targets[0][block]
+        listed[block * RAND : (block + 1) * RAND, :heads] = rand_ref[block]
     entries = listed[...].astype(jnp.float32).astype(jnp.bfloat16)
     for head in range(heads):
         cols = slice(head * HEAD_DIM, (head + 1) * HEAD_DIM)
-        packed_ref[head, :tokens, : 2 * HEAD_DIM] = jnp.concatenate(
-            (key_ref[:, cols], value_ref[:, cols]), axis=1
-        )
-        packed_ref[head, :tokens, 2 * HEAD_DIM :] = jnp.concatenate(
+        packed[head, :tokens] = jnp.concatenate((key_ref[:, cols], value_ref[:, cols]), axis=1)
+        packed[head, tokens : 2 * tokens] = jnp.concatenate(
             (query_ref[:, cols], grad_ref[:, cols]), axis=1
         )
-        packed_ref[head, tokens:, : 2 * HEAD_DIM] = entries
-        packed_ref[head, tokens:, 2 * HEAD_DIM :] = jnp.zeros_like(entries)
+        packed[head, 2 * tokens :] = entries
+        sends[head].start()
+    for send in sends:
+        send.wait()
 
 
 def unpack_kernel(packed_ref, attended_ref, query_ref, key_ref, value_ref):
-    heads = key_ref.shape[1] // HEAD_DIM
-    for head in range(heads):
+    tokens, width = key_ref.shape
+    for head in range(width // HEAD_DIM):
         cols = slice(head * HEAD_DIM, (head + 1) * HEAD_DIM)
-        for i, ref in enumerate((query_ref, attended_ref, key_ref, value_ref)):
-            ref[:, cols] = packed_ref[head, :, i * HEAD_DIM : (i + 1) * HEAD_DIM]
+        first, second = packed_ref[head, :tokens], packed_ref[head, tokens:]
+        query_ref[:, cols] = first[:, :HEAD_DIM]
+        attended_ref[:, cols] = first[:, HEAD_DIM:]
+        key_ref[:, cols] = second[:, :HEAD_DIM]
+        value_ref[:, cols] = second[:, HEAD_DIM:]
 
 
 def attend_kernel(
     pos_row_ref, pos_col_ref, x_ref, out_ref, acc, global_kv, global_acc, listed, starts, sem
 ):
-    shards, tokens, _ = out_ref.shape
+    shards = out_ref.shape[0]
+    tokens = out_ref.shape[1] // 2
     stride = x_ref.shape[0] // shards
     blocks = tokens // BLOCK
     global_count = pos_row_ref.shape[1]
     own = lax.axis_index("seq")
-    kv_cols = slice(0, 2 * HEAD_DIM)
-    rest_cols = slice(2 * HEAD_DIM, 4 * HEAD_DIM)
-
+
+    lists = jnp.zeros(listed.shape, jnp.float32)
+    list_lane = lax.broadcasted_iota(jnp.int32, listed.shape, 1)
     for shard in range(shards):
-        row = x_ref[shard * stride + tokens : (shard + 1) * stride, kv_cols].astype(jnp.float32)
-        passed = jnp.floor((row + 0.5) * (1.0 / blocks))
-        first = row * BLOCK + passed * (stride - tokens)
-        listed[shard] = first.astype(jnp.int32)
+        row = x_ref[shard * stride + 2 * tokens : (shard + 1) * stride].astype(jnp.float32)
+        entry = jnp.sum(jnp.where(list_lane == own, row, 0.0), axis=1, keepdims=True)
+        lists = jnp.where(list_lane == shard, entry, lists)
+    passed = jnp.floor((lists + 0.5) * (1.0 / blocks))
+    listed[...] = (lists * BLOCK + passed * (stride - tokens)).astype(jnp.int32)
     copy = pltpu.make_async_copy(listed, starts, sem)
     copy.start()
-    acc[...] = jnp.zeros_like(acc)
+    for shard in range(shards):
+        acc[shard * stride : shard * stride + tokens] = jnp.zeros(
+            (tokens, 2 * HEAD_DIM), jnp.float32
+        )
     global_acc[...] = jnp.zeros_like(global_acc)
-    place = lax.broadcasted_iota(jnp.int32, (global_count, shards * stride), 1)
-    pick = (place == pos_col_ref[...]).astype(jnp.bfloat16)
-    global_kv[...] = dot(pick, x_ref[:, kv_cols], 1, 0).astype(jnp.bfloat16)
+    picked = jnp.zeros((global_count, 2 * HEAD_DIM), jnp.float32)
+    for shard in range(shards):
+        place = shard * tokens + lax.broadcasted_iota(jnp.int32, (global_count, tokens), 1)
+        pick = (place == pos_col_ref[...]).astype(jnp.bfloat16)
+        picked = picked + dot(pick, x_ref[shard * stride : shard * stride + tokens], 1, 0)
+    global_kv[...] = picked.astype(jnp.bfloat16)
     copy.wait()
     lane = lax.broadcasted_iota(jnp.int32, (BLOCK, 6 * BLOCK), 1)
     half = lax.broadcasted_iota(jnp.int32, (BLOCK, 2 * HEAD_DIM), 1) < HEAD_DIM
@@ -342,22 +359,22 @@
 
     def products(shard):
         base = shard * stride
-        before = jnp.maximum(shard - 1, 0) * stride + (blocks - 1) * BLOCK
-        after = jnp.minimum(shard + 1, shards - 1) * stride
         rows = []
         for block in range(blocks):
-            rest = x_ref[at(base + block * BLOCK), rest_cols]
+            rest = x_ref[at(base + tokens + block * BLOCK)]
             rows += [rest * query_mask, rest * grad_mask]
         rows = jnp.concatenate(rows, axis=0)
         all_places, local_kvs, local_dots = [], [], []
         for block in range(blocks):
+            before = jnp.maximum(shard - 1, 0) * stride + (blocks - 1) * BLOCK
+            after = jnp.minimum(shard + 1, shards - 1) * stride
             places = [
                 base + (block - 1) * BLOCK if block else before,
                 base + block * BLOCK,
                 base + (block + 1) * BLOCK if block < blocks - 1 else after,
-            ] + [starts[shard, block * RAND + r, own] for r in range(RAND)]
+            ] + [starts[block * RAND + r, shard] for r in range(RAND)]
             all_places.append([at(p) for p in places])
-            local_kvs.append(jnp.concatenate([x_ref[p, kv_cols] for p in all_places[-1]], axis=0))
+            local_kvs.append(jnp.concatenate([x_ref[p] for p in all_places[-1]], axis=0))
             both = rows[2 * block * BLOCK : 2 * (block + 1) * BLOCK]
             local_dots.append(dot(both, local_kvs[-1], 1, 1))
         return rows, all_places, local_kvs, local_dots, dot(rows, global_kv[...], 1, 1)
@@ -420,7 +437,7 @@
                 grads.append(dot(side[block][0], rows[span], 0, 0))
             global_acc[...] += dot(global_side, rows, 0, 0)
             for block in range(blocks):
-                out_ref[shard, block * BLOCK : (block + 1) * BLOCK, kv_cols] = jnp.where(
+                out_ref[shard, block * BLOCK : (block + 1) * BLOCK] = jnp.where(
                     half,
                     results[block][:BLOCK] * (1.0 / math.sqrt(HEAD_DIM)),
                     results[block][BLOCK:],
@@ -432,54 +449,57 @@
     lax.fori_loop(0, shards // GROUP, shard_group, 0)
     global_grad = global_acc[...].astype(jnp.bfloat16)
     for shard in range(shards):
-        place = shard * stride + lax.broadcasted_iota(jnp.int32, (tokens, global_count), 0)
+        place = shard * tokens + lax.broadcasted_iota(jnp.int32, (tokens, global_count), 0)
         spread = (place == pos_row_ref[...]).astype(jnp.bfloat16)
-        out_ref[shard, :, rest_cols] = (
+        out_ref[shard, tokens:] = (
             acc[shard * stride : shard * stride + tokens] + dot(spread, global_grad, 1, 0)
         ).astype(jnp.bfloat16)
 
 
-def attend(whole, place):
-    shards, stride, _ = whole.shape
-    tokens = stride - listed_rows(stride - stride % BLOCK)
-    extra = stride - tokens
-    pair = 2 * HEAD_DIM
-    global_count = place.shape[0]
+def attend(whole, global_pos, tokens):
+    shards, stride, pair = whole.shape
+    lists = (stride - 2 * tokens, pair)
+    global_count = global_pos.shape[0]
     return pl.pallas_call(
         attend_kernel,
-        out_shape=jax.ShapeDtypeStruct((shards, tokens, 2 * pair), jnp.bfloat16),
+        out_shape=jax.ShapeDtypeStruct((shards, 2 * tokens, pair), jnp.bfloat16),
         scratch_shapes=[
             pltpu.VMEM((shards * stride, pair), jnp.float32),
             pltpu.VMEM((global_count, pair), jnp.bfloat16),
             pltpu.VMEM((global_count, pair), jnp.float32),
-            pltpu.VMEM((shards, extra, pair), jnp.int32),
-            pltpu.SMEM((shards, extra, pair), jnp.int32),
+            pltpu.VMEM(lists, jnp.int32),
+            pltpu.SMEM(lists, jnp.int32),
             pltpu.SemaphoreType.DMA,
         ],
         compiler_params=pltpu.CompilerParams(vmem_limit_bytes=VMEM_BYTES),
-    )(place.reshape(1, -1), place.reshape(-1, 1), whole.reshape(shards * stride, 2 * pair))
+    )(global_pos.reshape(1, -1), global_pos.reshape(-1, 1), whole.reshape(shards * stride, pair))
 
 
 def whole_body(queries, key_input, value_input, grad_output, rand_blocks, global_pos):
     tokens, width = queries.shape
     shards = lax.axis_size("seq")
     extra = listed_rows(tokens)
-    stride = tokens + extra
+    pair = 2 * HEAD_DIM
+    slots = (shards, 2 * tokens + extra, pair)
     narrow = jax.ShapeDtypeStruct((tokens, width), jnp.bfloat16)
+    anywhere = pl.BlockSpec(memory_space=pl.ANY)
     rand_lists = rand_blocks.transpose(0, 2, 1)
     packed = pl.pallas_call(
         pack_kernel,
-        out_shape=jax.ShapeDtypeStruct((shards, stride, 4 * HEAD_DIM), jnp.bfloat16),
-        in_specs=[pl.BlockSpec(memory_space=pl.ANY)] * 5,
+        out_shape=jax.ShapeDtypeStruct(slots, jnp.bfloat16),
+        in_specs=[anywhere] * 5,
+        out_specs=anywhere,
         scratch_shapes=[pltpu.VMEM(rand_lists.shape, jnp.int32)]
         + [pltpu.VMEM((tokens, width), jnp.bfloat16)] * 4
         + [
-            pltpu.VMEM((extra, 2 * HEAD_DIM), jnp.int32),
+            pltpu.VMEM((extra, pair), jnp.int32),
+            pltpu.VMEM(slots, jnp.bfloat16),
             pltpu.SemaphoreType.DMA((5,)),
+            pltpu.SemaphoreType.DMA((shards,)),
         ],
     )(rand_lists, key_input, value_input, queries, grad_output)
     whole = lax.all_to_all(packed, "seq", split_axis=0, concat_axis=0, tiled=True)
-    result = attend(whole, global_pos + global_pos // tokens * extra)
+    result = attend(whole, global_pos, tokens)
     returned = lax.all_to_all(result, "seq", split_axis=0, concat_axis=0, tiled=True)
     return pl.pallas_call(
         unpack_kernel,

time: 64.3 us -> 62.5 us (0.972)
  waiting for transfers between devices: 21.5 us -> 20.1 us
  Pallas kernels: 10.9 us -> 9.87 us
  local copies, waits for them, and re-layouts: 0.14 us -> 0.81 us
    all_to_all x1, waiting for transfers between devices: 21.5 us -> 20.1 us  [whole_body(): lax.all_to_all(packed, 'seq', split_axis=0, concat_axis=0, tiled=True)]
    pallas_call x2, Pallas kernels: 9.84 us -> 8.77 us  [the longest x1 6.52 us: attend(): pl.pallas_call(attend_kernel, out_shape=jax.ShapeDtypeStruct((shards, 2 *...]
    unnamed x2, local copies, waits for them, and re-layouts: 0.01 us -> 0.68 us
where the time goes in v4:
time: 62.5 us; the launch traced here: 62.3 us
  blocking collectives  23.6 us (38%)
  waiting for transfers between devices  20.1 us (32%)
  Pallas kernels  9.87 us (16%)
  starting transfers between devices  7.26 us (12%)
  local copies, waits for them, and re-layouts  0.81 us (1%)
  between operations  0.66 us (1%)
    all_to_all x1, blocking collectives, whole_body(): lax.all_to_all(result, 'seq', split_axis=0, concat_axis=0, tiled=True)  23.6 us
    all_to_all x1, waiting for transfers between devices, whole_body(): lax.all_to_all(packed, 'seq', split_axis=0, concat_axis=0, tiled=True)  20.1 us
    all_to_all x1, starting transfers between devices, whole_body(): lax.all_to_all(packed, 'seq', split_axis=0, concat_axis=0, tiled=True)  7.26 us
    pallas_call x1, Pallas kernels, attend(): pl.pallas_call(attend_kernel, out_shape=jax.ShapeDtypeStruct((shards, 2 *...  6.52 us
    pallas_call x1, Pallas kernels, whole_body(): pl.pallas_call(pack_kernel, out_shape=jax.ShapeDtypeStruct(slots, jnp.bfl...  2.25 us
  transfers between devices with their start and end apart: 1, of which 1 were waited for; matrix products, arithmetic and copies ran while one was open for 0% of the time, Pallas kernels for 0%

profile of v4, /device:TPU:0, one launch (start us, length us, event | category | flops | bytes accessed | tf_op | source)
XLA Modules:
  0.0 62.3 jit_solution(7342054229063304226)
XLA Ops:
  0.6 2.2 %shard_map.93 = bf16[8,400,128]{2,1,0:T(8,128)(2,1)} custom-call(s32[3,3,6]{2,1,0:T(4,128)} %bitcast.7, bf16[192,384]{1,0:T(8,128)(2,1)} %key_hbm.1, bf16[192,384]{1,0:T(8,128)(2,1)} %value_hbm.1, bf16[192,384]{1,0:T(8,128)(2,1)} %query_hbm.1, bf16[192,384]{1,0:T(8,128)(2,1)} %grad_hbm.1), custom_call_target="tpu_custom_call" | custom-call | tf_op jit(solution)/shard_map/pallas_call | solution.py:487
  2.9 7.3 %all-to-all-start = ((bf16[8,400,128]{2,1,0:T(8,128)(2,1)}), bf16[8,400,128]{2,1,0:T(8,128)(2,1)S(1)}, u32[]{:S(2)}, u32[]{:S(2)}) async-start(bf16[8,400,128]{2,1,0:T(8,128)(2,1)} %shard_map.93), calls=%async_computation | async-start | bytes 1638400 | tf_op jit(solution)/shard_map/all_to_all | solution.py:501
  10.2 0.0 copy-start
  10.2 0.7 %copy-done = s32[256]{0:T(256)S(1)} copy-done((s32[256]{0:T(256)S(1)}, s32[256]{0:T(256)}, u32[]{:S(2)}) %copy-start) | copy-done | bytes 1048
  10.8 0.1 copy.10.pos_col_ref
  11.0 20.1 %all-to-all-done = bf16[8,400,128]{2,1,0:T(8,128)(2,1)S(1)} async-done(((bf16[8,400,128]{2,1,0:T(8,128)(2,1)}), bf16[8,400,128]{2,1,0:T(8,128)(2,1)S(1)}, u32[]{:S(2)}, u32[]{:S(2)}) %all-to-all-start) | async-done | bytes 819232 | tf_op jit(solution)/shard_map/all_to_all | solution.py:501
  31.1 6.5 %shard_map.94 = bf16[8,384,128]{2,1,0:T(8,128)(2,1)S(1)} custom-call(s32[1,256]{1,0:T(1,128)S(1)} %bitcast.6, s32[256,1]{1,0:T(8,128)S(1)} %copy.10.pos_col_ref, bf16[3200,128]{1,0:T(8,128)(2,1)S(1)} %bitcast.4), custom_call_target="tpu_custom_call" | custom-call | tf_op jit(solution)/shard_map/pallas_call | solution.py:463
  37.6 23.6 %all_to_all.10.packed_ref = bf16[8,384,128]{2,1,0:T(8,128)(2,1)S(1)} all-to-all(bf16[8,384,128]{2,1,0:T(8,128)(2,1)S(1)} %shard_map.94), channel_id=1, replica_groups=mesh['groups'=2,'seq'=8,'head'=2] {'seq'}, dimensions={0} | all-to-all | bytes 1572864 | tf_op jit(solution)/shard_map/all_to_all | solution.py:503
  61.2 1.1 %shard_map.95 = (bf16[192,384]{1,0:T(8,128)(2,1)}, bf16[192,384]{1,0:T(8,128)(2,1)}, bf16[192,384]{1,0:T(8,128)(2,1)}, bf16[192,384]{1,0:T(8,128)(2,1)}) custom-call(bf16[8,384,128]{2,1,0:T(8,128)(2,1)S(1)} %all_to_all.10.packed_ref), custom_call_target="tpu_custom_call" | custom-call | tf_op jit(solution)/shard_map/pallas_call | solution.py:504
Async XLA Ops:
  2.9 28.2 %all-to-all-start = ((bf16[8,400,128]{2,1,0:T(8,128)(2,1)}), bf16[8,400,128]{2,1,0:T(8,128)(2,1)S(1)}, u32[]{:S(2)}, u32[]{:S(2)}) async-start(bf16[8,400,128]{2,1,0:T(8,128)(2,1)} %shard_map.93), calls=%async_computation | async-start | bytes 1638400 | tf_op jit(solution)/shard_map/all_to_all | solution.py:501
  10.2 0.7 %copy-start = (s32[256]{0:T(256)S(1)}, s32[256]{0:T(256)}, u32[]{:S(2)}) copy-start(s32[256]{0:T(256)} %param.11) | copy-start | bytes 3076

commit v5 on v4

--- a/solution.py
+++ b/solution.py
@@ -317,14 +317,20 @@
         value_ref[:, cols] = second[:, HEAD_DIM:]
 
 
+def places_kernel(pos_row_ref, pos_col_ref, pick_ref, spread_ref):
+    position = lax.broadcasted_iota(jnp.int32, pick_ref.shape, 1)
+    pick_ref[...] = (position == pos_col_ref[...]).astype(jnp.bfloat16)
+    position = lax.broadcasted_iota(jnp.int32, spread_ref.shape, 0)
+    spread_ref[...] = (position == pos_row_ref[...]).astype(jnp.bfloat16)
+
+
 def attend_kernel(
-    pos_row_ref, pos_col_ref, x_ref, out_ref, acc, global_kv, global_acc, listed, starts, sem
+    pick_ref, spread_ref, x_ref, out_ref, acc, global_kv, global_acc, listed, starts, sem
 ):
     shards = out_ref.shape[0]
     tokens = out_ref.shape[1] // 2
     stride = x_ref.shape[0] // shards
     blocks = tokens // BLOCK
-    global_count = pos_row_ref.shape[1]
     own = lax.axis_index("seq")
 
     lists = jnp.zeros(listed.shape, jnp.float32)
@@ -342,12 +348,10 @@
             (tokens, 2 * HEAD_DIM), jnp.float32
         )
     global_acc[...] = jnp.zeros_like(global_acc)
-    picked = jnp.zeros((global_count, 2 * HEAD_DIM), jnp.float32)
-    for shard in range(shards):
-        place = shard * tokens + lax.broadcasted_iota(jnp.int32, (global_count, tokens), 1)
-        pick = (place == pos_col_ref[...]).astype(jnp.bfloat16)
-        picked = picked + dot(pick, x_ref[shard * stride : shard * stride + tokens], 1, 0)
-    global_kv[...] = picked.astype(jnp.bfloat16)
+    all_kv = jnp.concatenate(
+        [x_ref[shard * stride : shard * stride + tokens] for shard in range(shards)], axis=0
+    )
+    global_kv[...] = dot(pick_ref[...], all_kv, 1, 0).astype(jnp.bfloat16)
     copy.wait()
     lane = lax.broadcasted_iota(jnp.int32, (BLOCK, 6 * BLOCK), 1)
     half = lax.broadcasted_iota(jnp.int32, (BLOCK, 2 * HEAD_DIM), 1) < HEAD_DIM
@@ -435,7 +439,7 @@
                 span = slice(2 * block * BLOCK, 2 * (block + 1) * BLOCK)
                 results.append(dot(side[block][0], local_kvs[block], 1, 0) + global_result[span])
                 grads.append(dot(side[block][0], rows[span], 0, 0))
-            global_acc[...] += dot(global_side, rows, 0, 0)
+            global_acc[...] += dot(rows, global_side, 0, 0)
             for block in range(blocks):
                 out_ref[shard, block * BLOCK : (block + 1) * BLOCK] = jnp.where(
                     half,
@@ -449,10 +453,9 @@
     lax.fori_loop(0, shards // GROUP, shard_group, 0)
     global_grad = global_acc[...].astype(jnp.bfloat16)
     for shard in range(shards):
-        place = shard * tokens + lax.broadcasted_iota(jnp.int32, (tokens, global_count), 0)
-        spread = (place == pos_row_ref[...]).astype(jnp.bfloat16)
+        spread = spread_ref[shard * tokens : (shard + 1) * tokens]
         out_ref[shard, tokens:] = (
-            acc[shard * stride : shard * stride + tokens] + dot(spread, global_grad, 1, 0)
+            acc[shard * stride : shard * stride + tokens] + dot(spread, global_grad, 1, 1)
         ).astype(jnp.bfloat16)
 
 
@@ -460,19 +463,32 @@
     shards, stride, pair = whole.shape
     lists = (stride - 2 * tokens, pair)
     global_count = global_pos.shape[0]
+    pick, spread = pl.pallas_call(
+        places_kernel,
+        out_shape=(
+            jax.ShapeDtypeStruct((global_count, shards * tokens), jnp.bfloat16),
+            jax.ShapeDtypeStruct((shards * tokens, global_count), jnp.bfloat16),
+        ),
+        compiler_params=pltpu.CompilerParams(vmem_limit_bytes=VMEM_BYTES),
+        cost_estimate=pl.CostEstimate(
+            flops=4 * shards * tokens * global_count,
+            bytes_accessed=4 * shards * tokens * global_count,
+            transcendentals=0,
+        ),
+    )(global_pos.reshape(1, -1), global_pos.reshape(-1, 1))
     return pl.pallas_call(
         attend_kernel,
         out_shape=jax.ShapeDtypeStruct((shards, 2 * tokens, pair), jnp.bfloat16),
         scratch_shapes=[
             pltpu.VMEM((shards * stride, pair), jnp.float32),
             pltpu.VMEM((global_count, pair), jnp.bfloat16),
-            pltpu.VMEM((global_count, pair), jnp.float32),
+            pltpu.VMEM((pair, global_count), jnp.float32),
             pltpu.VMEM(lists, jnp.int32),
             pltpu.SMEM(lists, jnp.int32),
             pltpu.SemaphoreType.DMA,
         ],
         compiler_params=pltpu.CompilerParams(vmem_limit_bytes=VMEM_BYTES),
-    )(global_pos.reshape(1, -1), global_pos.reshape(-1, 1), whole.reshape(shards * stride, pair))
+    )(pick, spread, whole.reshape(shards * stride, pair))
 
 
 def whole_body(queries, key_input, value_input, grad_output, rand_blocks, global_pos):

time: 62.5 us -> 62.2 us (level)
  transfers between devices with their start and end apart: 1 -> 1, of which waited for: 1 -> 1; matrix products, arithmetic and copies ran while one was open for 0% -> 0% of each run, Pallas kernels for 0% -> 1%
where the time goes in v5:
time: 62.2 us; the launch traced here: 62 us
  blocking collectives  23.6 us (38%)
  waiting for transfers between devices  19.5 us (31%)
  Pallas kernels  10.1 us (16%)
  starting transfers between devices  7.26 us (12%)
  local copies, waits for them, and re-layouts  0.81 us (1%)
  between operations  0.67 us (1%)
    all_to_all x1, blocking collectives, whole_body(): lax.all_to_all(result, 'seq', split_axis=0, concat_axis=0, tiled=True)  23.6 us
    all_to_all x1, waiting for transfers between devices, whole_body(): lax.all_to_all(packed, 'seq', split_axis=0, concat_axis=0, tiled=True)  19.5 us
    all_to_all x1, starting transfers between devices, whole_body(): lax.all_to_all(packed, 'seq', split_axis=0, concat_axis=0, tiled=True)  7.26 us
    pallas_call x1, Pallas kernels, attend(): pl.pallas_call(attend_kernel, out_shape=jax.ShapeDtypeStruct((shards, 2 *...  6.22 us
    pallas_call x1, Pallas kernels, whole_body(): pl.pallas_call(pack_kernel, out_shape=jax.ShapeDtypeStruct(slots, jnp.bfl...  2.26 us
  transfers between devices with their start and end apart: 1, of which 1 were waited for; matrix products, arithmetic and copies ran while one was open for 0% of the time, Pallas kernels for 1%

profile of v5, /device:TPU:0, one launch (start us, length us, event | category | flops | bytes accessed | tf_op | source)
XLA Modules:
  0.0 62.0 jit_solution(12966552535818792573)
XLA Ops:
  0.6 2.3 %shard_map.94 = bf16[8,400,128]{2,1,0:T(8,128)(2,1)} custom-call(s32[3,3,6]{2,1,0:T(4,128)} %bitcast.7, bf16[192,384]{1,0:T(8,128)(2,1)} %key_hbm.1, bf16[192,384]{1,0:T(8,128)(2,1)} %value_hbm.1, bf16[192,384]{1,0:T(8,128)(2,1)} %query_hbm.1, bf16[192,384]{1,0:T(8,128)(2,1)} %grad_hbm.1), custom_call_target="tpu_custom_call" | custom-call | tf_op jit(solution)/shard_map/pallas_call | solution.py:503
  2.9 7.3 %all-to-all-start = ((bf16[8,400,128]{2,1,0:T(8,128)(2,1)}), bf16[8,400,128]{2,1,0:T(8,128)(2,1)S(1)}, u32[]{:S(2)}, u32[]{:S(2)}) async-start(bf16[8,400,128]{2,1,0:T(8,128)(2,1)} %shard_map.94), calls=%async_computation | async-start | bytes 1638400 | tf_op jit(solution)/shard_map/all_to_all | solution.py:517
  10.2 0.0 copy-start
  10.2 0.7 %copy-done = s32[256]{0:T(256)S(1)} copy-done((s32[256]{0:T(256)S(1)}, s32[256]{0:T(256)}, u32[]{:S(2)}) %copy-start) | copy-done | bytes 1048
  10.8 0.1 copy.10.pos_col_ref
  11.0 0.5 shard_map.93
  11.5 19.5 %all-to-all-done = bf16[8,400,128]{2,1,0:T(8,128)(2,1)S(1)} async-done(((bf16[8,400,128]{2,1,0:T(8,128)(2,1)}), bf16[8,400,128]{2,1,0:T(8,128)(2,1)S(1)}, u32[]{:S(2)}, u32[]{:S(2)}) %all-to-all-start) | async-done | bytes 819232 | tf_op jit(solution)/shard_map/all_to_all | solution.py:517
  31.1 6.2 %shard_map.95 = bf16[8,384,128]{2,1,0:T(8,128)(2,1)S(1)} custom-call(bf16[256,1536]{1,0:T(8,128)(2,1)S(1)} %get-tuple-element.6.pick_ref, bf16[1536,256]{1,0:T(8,128)(2,1)S(1)} %get-tuple-element.7.spread_ref, bf16[3200,128]{1,0:T(8,128)(2,1)S(1)} %bitcast.4), custom_call_target="tpu_custom_call" | custom-call | tf_op jit(solution)/shard_map/pallas_call | solution.py:479
  37.3 23.6 %all_to_all.10.packed_ref = bf16[8,384,128]{2,1,0:T(8,128)(2,1)S(1)} all-to-all(bf16[8,384,128]{2,1,0:T(8,128)(2,1)S(1)} %shard_map.95), channel_id=1, replica_groups=mesh['groups'=2,'seq'=8,'head'=2] {'seq'}, dimensions={0} | all-to-all | bytes 1572864 | tf_op jit(solution)/shard_map/all_to_all | solution.py:519
  60.9 1.1 %shard_map.96 = (bf16[192,384]{1,0:T(8,128)(2,1)}, bf16[192,384]{1,0:T(8,128)(2,1)}, bf16[192,384]{1,0:T(8,128)(2,1)}, bf16[192,384]{1,0:T(8,128)(2,1)}) custom-call(bf16[8,384,128]{2,1,0:T(8,128)(2,1)S(1)} %all_to_all.10.packed_ref), custom_call_target="tpu_custom_call" | custom-call | tf_op jit(solution)/shard_map/pallas_call | solution.py:520
Async XLA Ops:
  2.9 28.2 %all-to-all-start = ((bf16[8,400,128]{2,1,0:T(8,128)(2,1)}), bf16[8,400,128]{2,1,0:T(8,128)(2,1)S(1)}, u32[]{:S(2)}, u32[]{:S(2)}) async-start(bf16[8,400,128]{2,1,0:T(8,128)(2,1)} %shard_map.94), calls=%async_computation | async-start | bytes 1638400 | tf_op jit(solution)/shard_map/all_to_all | solution.py:517
  10.2 0.7 %copy-start = (s32[256]{0:T(256)S(1)}, s32[256]{0:T(256)}, u32[]{:S(2)}) copy-start(s32[256]{0:T(256)} %param.11) | copy-start | bytes 3076

commit v6 on v5

--- a/solution.py
+++ b/solution.py
@@ -401,15 +401,15 @@
             jnp.sum(local_exp, axis=1, keepdims=True)
             + jnp.sum(global_exp, axis=1, keepdims=True)
         )
-        local_weight = (local_exp * inverse).astype(jnp.bfloat16)
-        global_weight = (global_exp * inverse).astype(jnp.bfloat16)
-        local_wf = local_weight.astype(jnp.float32)
-        global_wf = global_weight.astype(jnp.float32)
+        local_wf = local_exp * inverse
+        global_wf = global_exp * inverse
+        local_weight = local_wf.astype(jnp.bfloat16)
+        global_weight = global_wf.astype(jnp.bfloat16)
         delta = jnp.sum(local_wf * dp, axis=1, keepdims=True) + jnp.sum(
             global_wf * global_dp, axis=1, keepdims=True
         )
-        local_ds = (local_wf * (dp - delta)).astype(jnp.bfloat16)
-        global_ds = (global_wf * (global_dp - delta)).astype(jnp.bfloat16)
+        local_ds = local_weight * (dp - delta).astype(jnp.bfloat16)
+        global_ds = global_weight * (global_dp - delta).astype(jnp.bfloat16)
         return (
             jnp.concatenate((local_ds, local_weight), axis=0),
             jnp.concatenate((global_ds, global_weight), axis=0),

time: 62.2 us -> 62.1 us (level)
  no operation moved by 1% of the time
where the time goes in v6:
time: 62.1 us; the launch traced here: 61.8 us
  blocking collectives  23.6 us (38%)
  waiting for transfers between devices  19.5 us (31%)
  Pallas kernels  9.97 us (16%)
  starting transfers between devices  7.26 us (12%)
  local copies, waits for them, and re-layouts  0.81 us (1%)
  between operations  0.67 us (1%)
    all_to_all x1, blocking collectives, whole_body(): lax.all_to_all(result, 'seq', split_axis=0, concat_axis=0, tiled=True)  23.6 us
    all_to_all x1, waiting for transfers between devices, whole_body(): lax.all_to_all(packed, 'seq', split_axis=0, concat_axis=0, tiled=True)  19.5 us
    all_to_all x1, starting transfers between devices, whole_body(): lax.all_to_all(packed, 'seq', split_axis=0, concat_axis=0, tiled=True)  7.26 us
    pallas_call x1, Pallas kernels, attend(): pl.pallas_call(attend_kernel, out_shape=jax.ShapeDtypeStruct((shards, 2 *...  6.07 us
    pallas_call x1, Pallas kernels, whole_body(): pl.pallas_call(pack_kernel, out_shape=jax.ShapeDtypeStruct(slots, jnp.bfl...  2.26 us
  transfers between devices with their start and end apart: 1, of which 1 were waited for; matrix products, arithmetic and copies ran while one was open for 0% of the time, Pallas kernels for 1%

profile of v6, /device:TPU:0, one launch (start us, length us, event | category | flops | bytes accessed | tf_op | source)
XLA Modules:
  0.0 61.8 jit_solution(10063926226439052473)
XLA Ops:
  0.6 2.3 %shard_map.94 = bf16[8,400,128]{2,1,0:T(8,128)(2,1)} custom-call(s32[3,3,6]{2,1,0:T(4,128)} %bitcast.7, bf16[192,384]{1,0:T(8,128)(2,1)} %key_hbm.1, bf16[192,384]{1,0:T(8,128)(2,1)} %value_hbm.1, bf16[192,384]{1,0:T(8,128)(2,1)} %query_hbm.1, bf16[192,384]{1,0:T(8,128)(2,1)} %grad_hbm.1), custom_call_target="tpu_custom_call" | custom-call | tf_op jit(solution)/shard_map/pallas_call | solution.py:503
  2.9 7.3 %all-to-all-start = ((bf16[8,400,128]{2,1,0:T(8,128)(2,1)}), bf16[8,400,128]{2,1,0:T(8,128)(2,1)S(1)}, u32[]{:S(2)}, u32[]{:S(2)}) async-start(bf16[8,400,128]{2,1,0:T(8,128)(2,1)} %shard_map.94), calls=%async_computation | async-start | bytes 1638400 | tf_op jit(solution)/shard_map/all_to_all | solution.py:517
  10.2 0.0 copy-start
  10.2 0.7 %copy-done = s32[256]{0:T(256)S(1)} copy-done((s32[256]{0:T(256)S(1)}, s32[256]{0:T(256)}, u32[]{:S(2)}) %copy-start) | copy-done | bytes 1048
  10.8 0.1 copy.10.pos_col_ref
  11.0 0.5 shard_map.93
  11.5 19.5 %all-to-all-done = bf16[8,400,128]{2,1,0:T(8,128)(2,1)S(1)} async-done(((bf16[8,400,128]{2,1,0:T(8,128)(2,1)}), bf16[8,400,128]{2,1,0:T(8,128)(2,1)S(1)}, u32[]{:S(2)}, u32[]{:S(2)}) %all-to-all-start) | async-done | bytes 819232 | tf_op jit(solution)/shard_map/all_to_all | solution.py:517
  31.1 6.1 %shard_map.95 = bf16[8,384,128]{2,1,0:T(8,128)(2,1)S(1)} custom-call(bf16[256,1536]{1,0:T(8,128)(2,1)S(1)} %get-tuple-element.6.pick_ref, bf16[1536,256]{1,0:T(8,128)(2,1)S(1)} %get-tuple-element.7.spread_ref, bf16[3200,128]{1,0:T(8,128)(2,1)S(1)} %bitcast.4), custom_call_target="tpu_custom_call" | custom-call | tf_op jit(solution)/shard_map/pallas_call | solution.py:479
  37.2 23.6 %all_to_all.10.packed_ref = bf16[8,384,128]{2,1,0:T(8,128)(2,1)S(1)} all-to-all(bf16[8,384,128]{2,1,0:T(8,128)(2,1)S(1)} %shard_map.95), channel_id=1, replica_groups=mesh['groups'=2,'seq'=8,'head'=2] {'seq'}, dimensions={0} | all-to-all | bytes 1572864 | tf_op jit(solution)/shard_map/all_to_all | solution.py:519
  60.7 1.1 %shard_map.96 = (bf16[192,384]{1,0:T(8,128)(2,1)}, bf16[192,384]{1,0:T(8,128)(2,1)}, bf16[192,384]{1,0:T(8,128)(2,1)}, bf16[192,384]{1,0:T(8,128)(2,1)}) custom-call(bf16[8,384,128]{2,1,0:T(8,128)(2,1)S(1)} %all_to_all.10.packed_ref), custom_call_target="tpu_custom_call" | custom-call | tf_op jit(solution)/shard_map/pallas_call | solution.py:520
Async XLA Ops:
  2.9 28.2 %all-to-all-start = ((bf16[8,400,128]{2,1,0:T(8,128)(2,1)}), bf16[8,400,128]{2,1,0:T(8,128)(2,1)S(1)}, u32[]{:S(2)}, u32[]{:S(2)}) async-start(bf16[8,400,128]{2,1,0:T(8,128)(2,1)} %shard_map.94), calls=%async_computation | async-start | bytes 1638400 | tf_op jit(solution)/shard_map/all_to_all | solution.py:517
  10.2 0.7 %copy-start = (s32[256]{0:T(256)S(1)}, s32[256]{0:T(256)}, u32[]{:S(2)}) copy-start(s32[256]{0:T(256)} %param.11) | copy-start | bytes 3076
